TPU v7x, 32 devices: a whole 2x2x4 slice. The times are simulated.
32 devices in a mesh: shard: 16 (over z, y, core), tensor: 2 (over x).
Axes of the slice: x: 2, y: 2, z: 4, core: 2. Of those that a mesh axis runs over, the one named last changes fastest.
Arguments:
- grads: float32 [16, 2048, 1024], P(None, 'shard', 'tensor'), may hold values from -16 to 16
- momentum: bfloat16 [16, 2048, 1024], P(None, 'shard', 'tensor'), may hold values from -32 to 32
- counts: int32 [1], replicated, may hold values from 1 to 8
- emb_grad: float32 [8192, 2048], P('shard', 'tensor'), may hold values from -6 to 6
- emb_weight: float32 [8192, 2048], P('shard', 'tensor'), may hold values from -6 to 6
- emb_first: float32 [8192, 2048], P('shard', 'tensor'), may hold values from -2 to 2
- emb_second: float32 [8192, 2048], P('shard', 'tensor'), may hold values from 0.01 to 1
- gain_grad: float32 [16384], P(('shard', 'tensor')), may hold values from -6 to 6
- gain_weight: float32 [16384], P(('shard', 'tensor')), may hold values from 0.5 to 1.5
- gain_first: float32 [16384], P(('shard', 'tensor')), may hold values from -2 to 2
- gain_second: float32 [16384], P(('shard', 'tensor')), may hold values from 0.01 to 1
Outputs:
- new_momentum: bfloat16 [16, 2048, 1024], P(None, 'shard', 'tensor')
- update: float32 [16, 2048, 1024], P(None, 'shard', 'tensor')
- emb_weight_new: float32 [8192, 2048], P('shard', 'tensor')
- emb_first_new: float32 [8192, 2048], P('shard', 'tensor')
- emb_second_new: float32 [8192, 2048], P('shard', 'tensor')
- gain_weight_new: float32 [16384], P(('shard', 'tensor'))
- gain_first_new: float32 [16384], P(('shard', 'tensor'))
- gain_second_new: float32 [16384], P(('shard', 'tensor'))
All inputs are finite; a program needn't handle non-finite values.
Results may differ from a plain program's by a relative error of at most 0.012.
The roundings to bfloat16 on the way count: a program that leaves them out, or rounds other values in their place, can miss the bound.
Values may be sent and summed in bfloat16 or wider, within the bound.
No kernel may reach another device: no remote copies, remote signals or barrier semaphores. Data moves between devices by JAX's collectives and lax.ppermute only.
A program may use at most 128 MiB of HBM per device.

v0:
```python
import math

import jax
import jax.numpy as jnp
from jax import lax
from jax.sharding import PartitionSpec as P

D = 2048
NS_STEPS = 4


linear_coef = 3.4445
cubic_coef = -4.775
quintic_coef = 2.0315
momentum_rate = 0.95
learn_rate = 0.01
decay_weight = 0.1
first_rate = 0.9
second_rate = 0.95
adam_floor = 1e-08
norm_floor = 1e-07


def adamw(grad, weight, first, second, inverse):
    scaled = grad * inverse
    first_new = first_rate * first + (1.0 - first_rate) * scaled
    second_new = second_rate * second + (1.0 - second_rate) * scaled * scaled
    weight_new = weight - learn_rate * (
        first_new / (jnp.sqrt(second_new) + adam_floor) + decay_weight * weight
    )
    return (weight_new, first_new, second_new)


def combine(iterate, product, quintic, final):
    mixed = (
        linear_coef * iterate.astype(jnp.float32) + cubic_coef * product + quintic_coef * quintic
    )
    if final:
        return mixed * math.sqrt(D)
    return mixed.astype(jnp.bfloat16)


def columns_layout(iterate):
    for number in range(NS_STEPS):
        whole = lax.all_gather(iterate, "tensor", axis=1, tiled=True)
        gram = jnp.einsum("ri,rc->ic", whole, iterate, preferred_element_type=jnp.float32).astype(
            jnp.bfloat16
        )
        product = jnp.dot(whole, gram, preferred_element_type=jnp.float32)
        product_whole = lax.all_gather(product.astype(jnp.bfloat16), "tensor", axis=1, tiled=True)
        quintic = jnp.dot(product_whole, gram, preferred_element_type=jnp.float32)
        iterate = combine(iterate, product, quintic, number + 1 == NS_STEPS)
    return iterate


def body(
    grads,
    momentum,
    counts,
    emb_grad,
    emb_weight,
    emb_first,
    emb_second,
    gain_grad,
    gain_weight,
    gain_first,
    gain_second,
):
    inverse = 1.0 / counts[0].astype(jnp.float32)
    scaled = grads * inverse
    velocity = momentum_rate * momentum.astype(jnp.float32) + scaled
    advance = scaled + momentum_rate * velocity
    owned = lax.all_to_all(advance, "shard", split_axis=0, concat_axis=1, tiled=True)[0]
    total = jnp.sqrt(lax.psum(jnp.sum(owned * owned), "tensor"))
    iterate = (owned / (total + norm_floor)).astype(jnp.bfloat16)
    finished = columns_layout(iterate)
    blocks = finished.reshape(lax.axis_size("shard"), -1, finished.shape[1])
    update = lax.all_to_all(
        blocks.astype(jnp.bfloat16), "shard", split_axis=0, concat_axis=0, tiled=True
    ).astype(blocks.dtype)
    emb_new = adamw(emb_grad, emb_weight, emb_first, emb_second, inverse)
    gain_new = adamw(gain_grad, gain_weight, gain_first, gain_second, inverse)
    return (
        velocity.astype(jnp.bfloat16),
        update,
        emb_new[0],
        emb_new[1],
        emb_new[2],
        gain_new[0],
        gain_new[1],
        gain_new[2],
    )


def solution(mesh):
    placed = (
        P(None, "shard", "tensor"),
        P(None, "shard", "tensor"),
        P(),
        P("shard", "tensor"),
        P("shard", "tensor"),
        P("shard", "tensor"),
        P("shard", "tensor"),
        P(("shard", "tensor")),
        P(("shard", "tensor")),
        P(("shard", "tensor")),
        P(("shard", "tensor")),
    )
    return jax.shard_map(
        body,
        mesh=mesh,
        in_specs=placed,
        out_specs=(
            P(None, "shard", "tensor"),
            P(None, "shard", "tensor"),
            P("shard", "tensor"),
            P("shard", "tensor"),
            P("shard", "tensor"),
            P(("shard", "tensor")),
            P(("shard", "tensor")),
            P(("shard", "tensor")),
        ),
        check_vma=False,
    )
```

profile of v0, /device:TPU:12, one launch (start us, length us, event | category | flops | bytes accessed | tf_op | source)
XLA Modules:
  0.0 717.0 jit_solution(6828091837165881985)
XLA Ops:
  7.9 5.1 multiply_add_fusion
  13.0 98.1 %all_to_all.14 = f32[16,128,512]{2,1,0:T(8,128)S(1)} all-to-all(f32[16,128,512]{2,1,0:T(8,128)S(1)} %get-tuple-element.14), channel_id=1, replica_groups=mesh['shard'=16,'tensor'=2] {'shard'}, dimensions={0} | all-to-all | bytes 8388608 | tf_op jit(solution)/shard_map/all_to_all | solution.py:73
  111.1 2.0 copy-done
  113.1 1.7 multiply_reduce_fusion
  114.8 5.5 psum.7
  121.0 4.1 divide_convert_fusion
  125.2 57.2 %all-gather.9.cloned.1.call-done = bf16[2048,1024]{1,0:T(8,128)(2,1)} async-done(((bf16[2048,512]{1,0:T(8,128)(2,1)}), bf16[2048,1024]{1,0:T(8,128)(2,1)}) %all-gather.9.cloned.1.call-update) | async-done | bytes 4194320 | tf_op jit(solution)/shard_map/all_gather | solution.py:45
  182.4 5.4 convolution_convert_fusion.3
  187.8 5.2 fusion.5
  193.1 56.9 %all-gather.11.cloned.1.call-done = bf16[2048,1024]{1,0:T(8,128)(2,1)} async-done(((bf16[2048,512]{1,0:T(8,128)(2,1)}), bf16[2048,1024]{1,0:T(8,128)(2,1)}) %all-gather.11.cloned.1.call-update) | async-done | bytes 4194320 | tf_op jit(solution)/shard_map/all_gather | solution.py:50
  250.0 7.7 %add_convert_fusion.2 = bf16[2048,512]{1,0:T(8,128)(2,1)} fusion(f32[2048,512]{1,0:T(8,128)} %get-tuple-element.17, bf16[2048,512]{1,0:T(8,128)(2,1)S(1)} %bitcast.29, bf16[2048,1024]{1,0:T(8,128)(2,1)} %all-gather.11.cloned.1.call-done, bf16[1024,512]{1,0:T(8,128)(2,1)S(1)} %convolution_convert_fusion.3), kind=kOutput, calls=%fused_computation.3 | convolution fusion | flops 2154823680 | bytes 13631488 | tf_op jit(solution)/shard_map/dot_general | solution.py:51
  257.9 56.7 %all-gather.13.cloned.1.call-done = bf16[2048,1024]{1,0:T(8,128)(2,1)} async-done(((bf16[2048,512]{1,0:T(8,128)(2,1)}), bf16[2048,1024]{1,0:T(8,128)(2,1)}) %all-gather.13.cloned.1.call-update) | async-done | bytes 4194320 | tf_op jit(solution)/shard_map/all_gather | solution.py:45
  314.5 5.4 convolution_convert_fusion.2
  319.9 5.2 fusion.6
  325.2 56.9 %all-gather.15.cloned.1.call-done = bf16[2048,1024]{1,0:T(8,128)(2,1)} async-done(((bf16[2048,512]{1,0:T(8,128)(2,1)}), bf16[2048,1024]{1,0:T(8,128)(2,1)}) %all-gather.15.cloned.1.call-update) | async-done | bytes 4194320 | tf_op jit(solution)/shard_map/all_gather | solution.py:50
  382.0 7.7 %add_convert_fusion.1 = bf16[2048,512]{1,0:T(8,128)(2,1)} fusion(f32[2048,512]{1,0:T(8,128)} %get-tuple-element.19, bf16[2048,512]{1,0:T(8,128)(2,1)S(1)} %copy-done.2, bf16[2048,1024]{1,0:T(8,128)(2,1)} %all-gather.15.cloned.1.call-done, bf16[1024,512]{1,0:T(8,128)(2,1)S(1)} %convolution_convert_fusion.2), kind=kOutput, calls=%fused_computation.2 | convolution fusion | flops 2154823680 | bytes 13631488 | tf_op jit(solution)/shard_map/dot_general | solution.py:51
  389.8 56.9 %all-gather.17.cloned.1.call-done = bf16[2048,1024]{1,0:T(8,128)(2,1)} async-done(((bf16[2048,512]{1,0:T(8,128)(2,1)}), bf16[2048,1024]{1,0:T(8,128)(2,1)}) %all-gather.17.cloned.1.call-update) | async-done | bytes 4194320 | tf_op jit(solution)/shard_map/all_gather | solution.py:45
  446.6 5.4 convolution_convert_fusion.1
  452.0 5.2 fusion.7
  457.2 0.3 all-gather.21.cloned.1.call-start
  457.5 56.6 %all-gather.19.cloned.1.call-done = bf16[2048,1024]{1,0:T(8,128)(2,1)} async-done(((bf16[2048,512]{1,0:T(8,128)(2,1)}), bf16[2048,1024]{1,0:T(8,128)(2,1)}) %all-gather.19.cloned.1.call-update) | async-done | bytes 4194320 | tf_op jit(solution)/shard_map/all_gather | solution.py:50
  514.1 7.7 %add_convert_fusion = bf16[2048,512]{1,0:T(8,128)(2,1)} fusion(f32[2048,512]{1,0:T(8,128)} %get-tuple-element.21, bf16[2048,512]{1,0:T(8,128)(2,1)S(1)} %copy-done.3, bf16[2048,1024]{1,0:T(8,128)(2,1)} %all-gather.19.cloned.1.call-done, bf16[1024,512]{1,0:T(8,128)(2,1)S(1)} %convolution_convert_fusion.1), kind=kOutput, calls=%fused_computation.1 | convolution fusion | flops 2154823680 | bytes 13631488 | tf_op jit(solution)/shard_map/dot_general | solution.py:51
  521.9 56.9 %all-gather.21.cloned.1.call-done = bf16[2048,1024]{1,0:T(8,128)(2,1)} async-done(((bf16[2048,512]{1,0:T(8,128)(2,1)}), bf16[2048,1024]{1,0:T(8,128)(2,1)}) %all-gather.21.cloned.1.call-update) | async-done | bytes 4194320 | tf_op jit(solution)/shard_map/all_gather | solution.py:45
  578.7 5.4 convolution_convert_fusion
  584.1 5.2 fusion.8
  589.3 56.9 %all-gather.23.cloned.1.call-done = bf16[2048,1024]{1,0:T(8,128)(2,1)} async-done(((bf16[2048,512]{1,0:T(8,128)(2,1)}), bf16[2048,1024]{1,0:T(8,128)(2,1)}) %all-gather.23.cloned.1.call-update) | async-done | bytes 4194320 | tf_op jit(solution)/shard_map/all_gather | solution.py:50
  646.2 7.9 %multiply_convert_fusion = bf16[2048,512]{1,0:T(8,128)(2,1)} fusion(f32[2048,512]{1,0:T(8,128)} %get-tuple-element.23, bf16[2048,512]{1,0:T(8,128)(2,1)S(1)} %copy-done.4, bf16[2048,1024]{1,0:T(8,128)(2,1)} %all-gather.23.cloned.1.call-done, bf16[1024,512]{1,0:T(8,128)(2,1)S(1)} %convolution_convert_fusion), kind=kOutput, calls=%fused_computation | convolution fusion | flops 2155872256 | bytes 13631488 | tf_op jit(solution)/shard_map/dot_general | solution.py:51
  654.1 6.2 all-to-all-start.1
  660.4 0.6 multiply_subtract_fusion.1
  661.0 7.4 %multiply_subtract_fusion = (f32[512,1024]{1,0:T(8,128)}, f32[512,1024]{1,0:T(8,128)}, f32[512,1024]{1,0:T(8,128)}) fusion(f32[512,1024]{1,0:T(8,128)} %param.15, f32[512,1024]{1,0:T(8,128)} %param.14, f32[]{:T(128)} %bitcast, f32[512,1024]{1,0:T(8,128)} %param.17, f32[512,1024]{1,0:T(8,128)} %param.16), kind=kLoop, calls=%fused_computation.11 | loop fusion | flops 7340032 | bytes 14680068 | tf_op jit(solution)/shard_map/sub | solution.py:28
  668.4 39.2 %all-to-all-done.1 = bf16[16,128,512]{2,1,0:T(8,128)(2,1)S(1)} async-done(((bf16[16,128,512]{2,1,0:T(8,128)(2,1)}), bf16[16,128,512]{2,1,0:T(8,128)(2,1)S(1)}, u32[]{:S(2)}, u32[]{:S(2)}) %all-to-all-start.1) | async-done | bytes 2097184 | tf_op jit(solution)/shard_map/all_to_all | solution.py:78
  707.6 2.6 convert_element_type.92
  (40 shorter events, 0.7 us)
Async XLA Ops:
  7.2 175.3 %all-gather.9.cloned.1.call-start = ((), (), s32[]{:S(2)}) async-start(), calls=%async_computation.2 | async-start | bytes 6291456 | tf_op jit(solution)/shard_map/all_gather | solution.py:45
  111.1 2.0 copy-start
  125.2 124.8 %all-gather.11.cloned.1.call-start = ((), (), s32[]{:S(2)}) async-start(), calls=%async_computation.3 | async-start | bytes 6291456 | tf_op jit(solution)/shard_map/all_gather | solution.py:50
  182.4 5.4 copy-start.9
  187.8 62.1 %copy-start.1 = (bf16[16,128,512]{2,1,0:T(8,128)(2,1)S(1)}, bf16[16,128,512]{2,1,0:T(8,128)(2,1)}, u32[]{:S(2)}) copy-start(bf16[16,128,512]{2,1,0:T(8,128)(2,1)} %divide_convert_fusion) | copy-start | bytes 6291460
  193.0 121.5 %all-gather.13.cloned.1.call-start = ((), (), s32[]{:S(2)}) async-start(), calls=%async_computation.4 | async-start | bytes 6291456 | tf_op jit(solution)/shard_map/all_gather | solution.py:45
  257.6 124.4 %all-gather.15.cloned.1.call-start = ((), (), s32[]{:S(2)}) async-start(), calls=%async_computation.5 | async-start | bytes 6291456 | tf_op jit(solution)/shard_map/all_gather | solution.py:50
  314.5 5.4 copy-start.10
  319.9 62.1 %copy-start.2 = (bf16[2048,512]{1,0:T(8,128)(2,1)S(1)}, bf16[2048,512]{1,0:T(8,128)(2,1)}, u32[]{:S(2)}) copy-start(bf16[2048,512]{1,0:T(8,128)(2,1)} %add_convert_fusion.2) | copy-start | bytes 6291460
  325.1 121.5 %all-gather.17.cloned.1.call-start = ((), (), s32[]{:S(2)}) async-start(), calls=%async_computation.6 | async-start | bytes 6291456 | tf_op jit(solution)/shard_map/all_gather | solution.py:45
  389.7 124.4 %all-gather.19.cloned.1.call-start = ((), (), s32[]{:S(2)}) async-start(), calls=%async_computation.7 | async-start | bytes 6291456 | tf_op jit(solution)/shard_map/all_gather | solution.py:50
  446.6 5.4 copy-start.11
  452.0 62.1 %copy-start.3 = (bf16[2048,512]{1,0:T(8,128)(2,1)S(1)}, bf16[2048,512]{1,0:T(8,128)(2,1)}, u32[]{:S(2)}) copy-start(bf16[2048,512]{1,0:T(8,128)(2,1)} %add_convert_fusion.1) | copy-start | bytes 6291460
  457.2 121.5 %all-gather.21.cloned.1.call-start = ((), (), s32[]{:S(2)}) async-start(), calls=%async_computation.8 | async-start | bytes 6291456 | tf_op jit(solution)/shard_map/all_gather | solution.py:45
  521.8 124.4 %all-gather.23.cloned.1.call-start = ((), (), s32[]{:S(2)}) async-start(), calls=%async_computation.9 | async-start | bytes 6291456 | tf_op jit(solution)/shard_map/all_gather | solution.py:50
  578.7 5.4 copy-start.12
  584.1 62.1 %copy-start.4 = (bf16[2048,512]{1,0:T(8,128)(2,1)S(1)}, bf16[2048,512]{1,0:T(8,128)(2,1)}, u32[]{:S(2)}) copy-start(bf16[2048,512]{1,0:T(8,128)(2,1)} %add_convert_fusion) | copy-start | bytes 6291460
  654.1 6.2 copy-start.5
  654.1 6.2 copy-start.6
  654.1 6.2 copy-start.7
  654.1 6.2 copy-start.8
  654.1 53.5 %all-to-all-start.1 = ((bf16[16,128,512]{2,1,0:T(8,128)(2,1)}), bf16[16,128,512]{2,1,0:T(8,128)(2,1)S(1)}, u32[]{:S(2)}, u32[]{:S(2)}) async-start(bf16[16,128,512]{2,1,0:T(8,128)(2,1)} %bitcast.30), calls=%async_computation.1 | async-start | bytes 4194304 | tf_op jit(solution)/shard_map/all_to_all | solution.py:78
Sparse Core Ops, SparseCore 0:
  125.3 57.0 all-gather.8
  193.2 56.7 all-gather.10
  257.7 56.7 all-gather.12
  325.3 56.7 all-gather.14
  389.8 56.7 all-gather.16
  457.3 56.7 all-gather.18
  521.9 56.7 all-gather.20
  589.4 56.7 all-gather.22
where the time goes:
time: 718 us; the launch traced here: 717 us
  waiting for transfers between devices  494 us (69%)
  blocking collectives  104 us (14%)
  matrix products  73 us (10%)
  other arithmetic  21.5 us (3%)
  between operations  15.7 us (2%)
    all_gather x4, waiting for transfers between devices, columns_layout(): whole = lax.all_gather(iterate, 'tensor', axis=1, tiled=True)  228 us
    all_gather x4, waiting for transfers between devices, columns_layout(): lax.all_gather(product.astype(jnp.bfloat16), 'tensor', axis=1, tiled=True)  227 us
    all_to_all x1, blocking collectives, body(): lax.all_to_all(advance, 'shard', split_axis=0, concat_axis=1, tiled=True)[0]  98.1 us
    all_to_all x1, waiting for transfers between devices, body(): lax.all_to_all(blocks.astype(jnp.bfloat16), 'shard', split_axis=0, concat...  39.2 us
    dot_general x4, matrix products, columns_layout(): quintic = jnp.dot(product_whole, gram, preferred_element_type=jnp.float32)  30.8 us
    dot_general x4, matrix products, columns_layout(): jnp.einsum('ri,rc->ic', whole, iterate, preferred_element_type=jnp.float32)  21.4 us
    dot_general x4, matrix products, columns_layout(): product = jnp.dot(whole, gram, preferred_element_type=jnp.float32)  20.8 us
  transfers between devices with their start and end apart: 9, of which 9 were waited for; matrix products, arithmetic and copies ran while one was open for 1% of the time, Pallas kernels for 0%

commit v1 on v0

--- a/solution.py
+++ b/solution.py
@@ -1,13 +1,18 @@
+import functools
 import math
 
 import jax
 import jax.numpy as jnp
 from jax import lax
+from jax.experimental import pallas as pl
+from jax.experimental.pallas import tpu as pltpu
 from jax.sharding import PartitionSpec as P
 
 D = 2048
 NS_STEPS = 4
-
+CORES = 2
+EDGE = 256
+LIFT = 512.0
 
 linear_coef = 3.4445
 cubic_coef = -4.775
@@ -31,26 +36,139 @@
     return (weight_new, first_new, second_new)
 
 
-def combine(iterate, product, quintic, final):
-    mixed = (
-        linear_coef * iterate.astype(jnp.float32) + cubic_coef * product + quintic_coef * quintic
-    )
-    if final:
-        return mixed * math.sqrt(D)
-    return mixed.astype(jnp.bfloat16)
-
-
-def columns_layout(iterate):
-    for number in range(NS_STEPS):
-        whole = lax.all_gather(iterate, "tensor", axis=1, tiled=True)
-        gram = jnp.einsum("ri,rc->ic", whole, iterate, preferred_element_type=jnp.float32).astype(
-            jnp.bfloat16
-        )
-        product = jnp.dot(whole, gram, preferred_element_type=jnp.float32)
-        product_whole = lax.all_gather(product.astype(jnp.bfloat16), "tensor", axis=1, tiled=True)
-        quintic = jnp.dot(product_whole, gram, preferred_element_type=jnp.float32)
-        iterate = combine(iterate, product, quintic, number + 1 == NS_STEPS)
-    return iterate
+def span(index):
+    return slice(index * EDGE, (index + 1) * EDGE)
+
+
+def upper_blocks(width):
+    return [(i, j) for j in range(width // EDGE) for i in range(j + 1)]
+
+
+def write_gram(turned_ref, gram_ref):
+    slot = 0
+    for j in range(turned_ref.shape[0] // EDGE):
+        part = lax.dot_general(
+            turned_ref[: (j + 1) * EDGE, :],
+            turned_ref[span(j), :],
+            (((1,), (1,)), ((), ())),
+            preferred_element_type=jnp.float32,
+        )
+        for i in range(j + 1):
+            gram_ref[slot] = part[span(i), :].astype(jnp.bfloat16)
+            slot += 1
+
+
+def write_poly(own_ref, other_ref, gram, poly):
+    for slot, (i, j) in enumerate(upper_blocks(gram.shape[0])):
+        block = own_ref[slot].astype(jnp.float32) + other_ref[slot].astype(jnp.float32)
+        block = block.astype(jnp.bfloat16)
+        gram[span(i), span(j)] = block
+        if i != j:
+            gram[span(j), span(i)] = block.T
+    for j in range(gram.shape[0] // EDGE):
+        square = jnp.dot(
+            gram[: (j + 1) * EDGE, :], gram[:, span(j)], preferred_element_type=jnp.float32
+        )
+        for i in range(j + 1):
+            block = cubic_coef * gram[span(i), span(j)].astype(jnp.float32)
+            block = (block + quintic_coef * square[span(i), :]).astype(jnp.bfloat16)
+            poly[span(i), span(j)] = block
+            if i != j:
+                poly[span(j), span(i)] = block.T
+
+
+def first_kernel(block_ref, turned_ref, gram_ref, *, tensor):
+    blocks, rows, cols = block_ref.shape
+    for s in range(blocks // tensor):
+        for t in range(tensor):
+            turned_ref[t * cols : (t + 1) * cols, s * rows : (s + 1) * rows] = block_ref[
+                s * tensor + t
+            ].T
+    write_gram(turned_ref, gram_ref)
+
+
+def middle_kernel(turned_ref, own_ref, other_ref, next_ref, gram_ref, gram, poly):
+    write_poly(own_ref, other_ref, gram, poly)
+    for c in range(turned_ref.shape[1] // EDGE):
+        old = turned_ref[:, span(c)]
+        new = linear_coef * old.astype(jnp.float32) + jnp.dot(
+            poly[...], old, preferred_element_type=jnp.float32
+        )
+        next_ref[:, span(c)] = new.astype(jnp.bfloat16)
+    write_gram(next_ref, gram_ref)
+
+
+def last_kernel(turned_ref, own_ref, other_ref, block_ref, gram, poly, *, tensor):
+    write_poly(own_ref, other_ref, gram, poly)
+    blocks, rows, cols = block_ref.shape
+    for s in range(blocks // tensor):
+        old = turned_ref[:, s * rows : (s + 1) * rows].T
+        new = linear_coef * old.astype(jnp.float32) + jnp.dot(
+            old, poly[...], preferred_element_type=jnp.float32
+        )
+        new = (math.sqrt(D) * new).astype(jnp.bfloat16)
+        for t in range(tensor):
+            block_ref[s * tensor + t] = new[:, t * cols : (t + 1) * cols]
+
+
+def run_kernel(kernel, results, scratch, *operands):
+    whole = pl.BlockSpec(memory_space=pltpu.VMEM)
+    return pl.pallas_call(
+        kernel,
+        out_shape=results,
+        in_specs=[whole] * len(operands),
+        out_specs=[whole] * len(results),
+        scratch_shapes=scratch,
+        compiler_params=pltpu.CompilerParams(vmem_limit_bytes=48 * 2**20),
+    )(*operands)
+
+
+def other_core(value):
+    shards = lax.axis_size("shard")
+    return lax.ppermute(value, "shard", [(i, i ^ 1) for i in range(shards)])
+
+
+def chip_groups():
+    shards, tensor = lax.axis_size("shard"), lax.axis_size("tensor")
+    return [
+        [s * tensor + t for s in range(core, shards, CORES) for t in range(tensor)]
+        for core in range(CORES)
+    ]
+
+
+def exchange(blocks):
+    return lax.all_to_all(
+        blocks,
+        ("shard", "tensor"),
+        split_axis=0,
+        concat_axis=0,
+        axis_index_groups=chip_groups(),
+        tiled=True,
+    )
+
+
+def orthogonalize(blocks):
+    tensor = lax.axis_size("tensor")
+    width = tensor * blocks.shape[2]
+    height = blocks.shape[0] // tensor * blocks.shape[1]
+    turned_type = jax.ShapeDtypeStruct((width, height), jnp.bfloat16)
+    gram_type = jax.ShapeDtypeStruct((len(upper_blocks(width)), EDGE, EDGE), jnp.bfloat16)
+    squares = [pltpu.VMEM((width, width), jnp.bfloat16)] * 2
+    turned, own = run_kernel(
+        functools.partial(first_kernel, tensor=tensor), [turned_type, gram_type], [], blocks
+    )
+    for _ in range(NS_STEPS - 1):
+        turned, own = run_kernel(
+            middle_kernel, [turned_type, gram_type], squares, turned, own, other_core(own)
+        )
+    return run_kernel(
+        functools.partial(last_kernel, tensor=tensor),
+        [jax.ShapeDtypeStruct(blocks.shape, jnp.bfloat16)],
+        squares,
+        turned,
+        own,
+        other_core(own),
+    )[0]
 
 
 def body(
@@ -70,14 +188,11 @@
     scaled = grads * inverse
     velocity = momentum_rate * momentum.astype(jnp.float32) + scaled
     advance = scaled + momentum_rate * velocity
-    owned = lax.all_to_all(advance, "shard", split_axis=0, concat_axis=1, tiled=True)[0]
-    total = jnp.sqrt(lax.psum(jnp.sum(owned * owned), "tensor"))
+    owned = exchange((advance * LIFT).astype(jnp.float16)).astype(jnp.float32) / LIFT
+    total = jnp.sum(owned * owned)
+    total = jnp.sqrt(total + other_core(total))
     iterate = (owned / (total + norm_floor)).astype(jnp.bfloat16)
-    finished = columns_layout(iterate)
-    blocks = finished.reshape(lax.axis_size("shard"), -1, finished.shape[1])
-    update = lax.all_to_all(
-        blocks.astype(jnp.bfloat16), "shard", split_axis=0, concat_axis=0, tiled=True
-    ).astype(blocks.dtype)
+    update = exchange(orthogonalize(iterate)).astype(jnp.float32)
     emb_new = adamw(emb_grad, emb_weight, emb_first, emb_second, inverse)
     gain_new = adamw(gain_grad, gain_weight, gain_first, gain_second, inverse)
     return (

time: 718 us -> 172 us (0.24)
  waiting for transfers between devices: 494 us -> 53.1 us
  matrix products: 73 us -> 0 us
  blocking collectives: 104 us -> 54.6 us
  Pallas kernels: 0 us -> 31.5 us
  between operations: 15.7 us -> 2.68 us
    all_gather x8 -> x0, waiting for transfers between devices: 455 us -> none  [the longest x4 228 us: columns_layout(): whole = lax.all_gather(iterate, 'tensor', axis=1, tiled=True)]
    dot_general x12 -> x0, matrix products: 73 us -> none  [the longest x4 30.8 us: columns_layout(): quintic = jnp.dot(product_whole, gram, preferred_element_type=jnp.float32)]
    all_to_all x1, blocking collectives: 98.1 us -> 54.6 us  [exchange(): lax.all_to_all(blocks, ('shard', 'tensor'), split_axis=0, concat_axis=0,...]
    pallas_call x0 -> x5, Pallas kernels: none -> 31.5 us  [run_kernel(): pl.pallas_call(kernel, out_shape=results, in_specs=[whole] * len(operands...]
    ppermute x0 -> x5, waiting for transfers between devices: none -> 12.7 us  [other_core(): return lax.ppermute(value, 'shard', [(i, i ^ 1) for i in range(shards)])]
  transfers between devices with their start and end apart: 9 -> 6, of which waited for: 9 -> 6; matrix products, arithmetic and copies ran while one was open for 1% -> 5% of each run, Pallas kernels for 0% -> 0%
where the time goes in v1:
time: 172 us; the launch traced here: 171 us
  blocking collectives  54.6 us (32%)
  waiting for transfers between devices  53.1 us (31%)
  Pallas kernels  31.5 us (18%)
  other arithmetic  18.2 us (11%)
  starting transfers between devices  6.09 us (4%)
  local copies, waits for them, and re-layouts  5.27 us (3%)
  between operations  2.68 us (2%)
    all_to_all x1, blocking collectives, exchange(): lax.all_to_all(blocks, ('shard', 'tensor'), split_axis=0, concat_axis=0,...  54.6 us
    all_to_all x1, waiting for transfers between devices, exchange(): lax.all_to_all(blocks, ('shard', 'tensor'), split_axis=0, concat_axis=0,...  40.4 us
    pallas_call x5, Pallas kernels, run_kernel(): pl.pallas_call(kernel, out_shape=results, in_specs=[whole] * len(operands...  31.5 us
    ppermute x5, waiting for transfers between devices, other_core(): return lax.ppermute(value, 'shard', [(i, i ^ 1) for i in range(shards)])  12.7 us
    sub x2, other arithmetic, adamw(): weight - learn_rate * (first_new / (jnp.sqrt(second_new) + adam_floor) +...  8.03 us
    convert_element_type x1, other arithmetic, body(): (advance * LIFT).astype(jnp.float16)  5.38 us
    unnamed x16, local copies, waits for them, and re-layouts  5.27 us
    all_to_all x1, starting transfers between devices, exchange(): lax.all_to_all(blocks, ('shard', 'tensor'), split_axis=0, concat_axis=0,...  5.26 us
  transfers between devices with their start and end apart: 6, of which 6 were waited for; matrix products, arithmetic and copies ran while one was open for 5% of the time, Pallas kernels for 0%

profile of v1, /device:TPU:12, one launch (start us, length us, event | category | flops | bytes accessed | tf_op | source)
XLA Modules:
  0.0 171.4 jit_solution(5116949667071208486)
XLA Ops:
  1.3 5.4 %multiply_convert_fusion = (f16[16,128,512]{2,1,0:T(8,128)(2,1)S(1)}, bf16[16,128,512]{2,1,0:T(8,128)(2,1)}) fusion(bf16[16,128,512]{2,1,0:T(8,128)(2,1)} %param.12, f32[16,128,512]{2,1,0:T(8,128)} %param.11, f32[]{:T(128)} %bitcast), kind=kLoop, calls=%fused_computation.3 | loop fusion | flops 9437184 | bytes 10485764 | tf_op jit(solution)/shard_map/convert_element_type | solution.py:191
  6.7 54.6 %all_to_all.10 = f16[16,128,512]{2,1,0:T(8,128)(2,1)S(1)} all-to-all(f16[16,128,512]{2,1,0:T(8,128)(2,1)S(1)} %get-tuple-element.30), channel_id=1, replica_groups={{0,1,4,5,8,9,12,13,16,17,20,21,24,25,28,29},{2,3,6,7,10,11,14,15,18,19,..., dimensions={0} | all-to-all | bytes 4194304 | tf_op jit(solution)/shard_map/all_to_all | solution.py:140
  61.3 1.7 multiply_reduce_fusion
  63.0 0.0 collective-permute-start
  63.0 1.4 collective-permute-done
  65.6 0.5 divide_convert_fusion.block_ref
  66.1 1.7 %shard_map.170 = (bf16[1024,1024]{1,0:T(8,128)(2,1)S(1)}, bf16[10,256,256]{2,1,0:T(8,128)(2,1)S(1)}) custom-call(bf16[16,128,512]{2,1,0:T(8,128)(2,1)S(1)} %divide_convert_fusion.block_ref), custom_call_target="tpu_custom_call" | custom-call | tf_op jit(solution)/shard_map/pallas_call | solution.py:116
  67.9 0.0 copy-start.2
  67.9 1.3 copy-done.2
  69.2 0.2 collective-permute-start.1
  69.4 2.8 %collective-permute-done.1.other_ref = bf16[10,256,256]{2,1,0:T(8,128)(2,1)S(1)} collective-permute-done((bf16[10,256,256]{2,1,0:T(8,128)(2,1)S(1)}, bf16[10,256,256]{2,1,0:T(8,128)(2,1)S(1)}, u32[]{:S(2)}, u32[]{:S(2)}) %collective-permute-start.1) | collective-permute-done | bytes 1310752 | tf_op jit(solution)/shard_map/ppermute | solution.py:128
  72.2 7.5 %shard_map.171 = (bf16[1024,1024]{1,0:T(8,128)(2,1)S(1)}, bf16[10,256,256]{2,1,0:T(8,128)(2,1)S(1)}) custom-call(bf16[1024,1024]{1,0:T(8,128)(2,1)} %copy-done.2, bf16[10,256,256]{2,1,0:T(8,128)(2,1)S(1)} %get-tuple-element.17.own_ref, bf16[10,256,256]{2,1,0:T(8,128)(2,1)S(1)} %collective-permute-done.1.other_ref), custom_call_target="tpu_custom_call" | custom-call | tf_op jit(solution)/shard_map/pallas_call | solution.py:116
  79.7 0.0 copy-start
  79.7 1.3 copy-done
  81.0 0.2 collective-permute-start.2
  81.2 2.8 %collective-permute-done.2.other_ref = bf16[10,256,256]{2,1,0:T(8,128)(2,1)S(1)} collective-permute-done((bf16[10,256,256]{2,1,0:T(8,128)(2,1)S(1)}, bf16[10,256,256]{2,1,0:T(8,128)(2,1)S(1)}, u32[]{:S(2)}, u32[]{:S(2)}) %collective-permute-start.2) | collective-permute-done | bytes 1310752 | tf_op jit(solution)/shard_map/ppermute | solution.py:128
  84.1 7.7 %shard_map.172 = (bf16[1024,1024]{1,0:T(8,128)(2,1)S(1)}, bf16[10,256,256]{2,1,0:T(8,128)(2,1)S(1)}) custom-call(bf16[1024,1024]{1,0:T(8,128)(2,1)} %copy-done, bf16[10,256,256]{2,1,0:T(8,128)(2,1)S(1)} %get-tuple-element.19.own_ref, bf16[10,256,256]{2,1,0:T(8,128)(2,1)S(1)} %collective-permute-done.2.other_ref), custom_call_target="tpu_custom_call" | custom-call | tf_op jit(solution)/shard_map/pallas_call | solution.py:116
  91.7 0.0 copy-start.1
  91.7 1.3 copy-done.1
  93.1 0.2 collective-permute-start.3
  93.3 2.8 %collective-permute-done.3.other_ref = bf16[10,256,256]{2,1,0:T(8,128)(2,1)S(1)} collective-permute-done((bf16[10,256,256]{2,1,0:T(8,128)(2,1)S(1)}, bf16[10,256,256]{2,1,0:T(8,128)(2,1)S(1)}, u32[]{:S(2)}, u32[]{:S(2)}) %collective-permute-start.3) | collective-permute-done | bytes 1310752 | tf_op jit(solution)/shard_map/ppermute | solution.py:128
  96.1 7.5 %shard_map.173 = (bf16[1024,1024]{1,0:T(8,128)(2,1)S(1)}, bf16[10,256,256]{2,1,0:T(8,128)(2,1)S(1)}) custom-call(bf16[1024,1024]{1,0:T(8,128)(2,1)} %copy-done.1, bf16[10,256,256]{2,1,0:T(8,128)(2,1)S(1)} %get-tuple-element.21.own_ref, bf16[10,256,256]{2,1,0:T(8,128)(2,1)S(1)} %collective-permute-done.3.other_ref), custom_call_target="tpu_custom_call" | custom-call | tf_op jit(solution)/shard_map/pallas_call | solution.py:116
  103.6 0.0 copy-start.3
  103.6 1.3 copy-done.3
  104.9 0.2 collective-permute-start.4
  105.1 2.8 %collective-permute-done.4.other_ref = bf16[10,256,256]{2,1,0:T(8,128)(2,1)S(1)} collective-permute-done((bf16[10,256,256]{2,1,0:T(8,128)(2,1)S(1)}, bf16[10,256,256]{2,1,0:T(8,128)(2,1)S(1)}, u32[]{:S(2)}, u32[]{:S(2)}) %collective-permute-start.4) | collective-permute-done | bytes 1310752 | tf_op jit(solution)/shard_map/ppermute | solution.py:128
  107.9 7.1 %shard_map.174 = bf16[16,128,512]{2,1,0:T(8,128)(2,1)} custom-call(bf16[1024,1024]{1,0:T(8,128)(2,1)} %copy-done.3, bf16[10,256,256]{2,1,0:T(8,128)(2,1)S(1)} %get-tuple-element.23.own_ref, bf16[10,256,256]{2,1,0:T(8,128)(2,1)S(1)} %collective-permute-done.4.other_ref), custom_call_target="tpu_custom_call" | custom-call | tf_op jit(solution)/shard_map/pallas_call | solution.py:116
  115.1 5.3 %all-to-all-start.1 = ((bf16[16,128,512]{2,1,0:T(8,128)(2,1)}), bf16[16,128,512]{2,1,0:T(8,128)(2,1)S(1)}, u32[]{:S(2)}, u32[]{:S(2)}) async-start(bf16[16,128,512]{2,1,0:T(8,128)(2,1)} %shard_map.174), calls=%async_computation.1 | async-start | bytes 4194304 | tf_op jit(solution)/shard_map/all_to_all | solution.py:140
  120.4 0.6 multiply_subtract_fusion.1
  121.0 7.4 %multiply_subtract_fusion = (f32[512,1024]{1,0:T(8,128)}, f32[512,1024]{1,0:T(8,128)}, f32[512,1024]{1,0:T(8,128)}) fusion(f32[512,1024]{1,0:T(8,128)} %param.15, f32[512,1024]{1,0:T(8,128)} %param.14, f32[]{:T(128)} %bitcast, f32[512,1024]{1,0:T(8,128)} %param.17, f32[512,1024]{1,0:T(8,128)} %param.16), kind=kLoop, calls=%fused_computation.8 | loop fusion | flops 7340032 | bytes 14680068 | tf_op jit(solution)/shard_map/sub | solution.py:33
  128.4 40.4 %all-to-all-done.1 = bf16[16,128,512]{2,1,0:T(8,128)(2,1)S(1)} async-done(((bf16[16,128,512]{2,1,0:T(8,128)(2,1)}), bf16[16,128,512]{2,1,0:T(8,128)(2,1)S(1)}, u32[]{:S(2)}, u32[]{:S(2)}) %all-to-all-start.1) | async-done | bytes 2097184 | tf_op jit(solution)/shard_map/all_to_all | solution.py:140
  168.8 2.6 %convert_element_type.28 = f32[16,128,512]{2,1,0:T(8,128)} convert(bf16[16,128,512]{2,1,0:T(8,128)(2,1)S(1)} %all-to-all-done.1) | non-fusion elementwise | flops 1048576 | bytes 6291456 | tf_op jit(solution)/shard_map/convert_element_type | solution.py:195
  (8 shorter events, 0.0 us)
Async XLA Ops:
  63.0 1.4 collective-permute-start
  67.9 1.3 copy-start.2
  69.2 3.0 %collective-permute-start.1 = (bf16[10,256,256]{2,1,0:T(8,128)(2,1)S(1)}, bf16[10,256,256]{2,1,0:T(8,128)(2,1)S(1)}, u32[]{:S(2)}, u32[]{:S(2)}) collective-permute-start(bf16[10,256,256]{2,1,0:T(8,128)(2,1)S(1)} %get-tuple-element.17.own_ref), channel_id=1, source_target_pairs={{0,2},{2,0},{4,6},{6,4},{8,10},{10,8},{12,14},{14,12},{16,18},{18,... | collective-permute-start | bytes 3932168 | tf_op jit(solution)/shard_map/ppermute | solution.py:128
  79.7 1.3 copy-start
  81.0 3.0 %collective-permute-start.2 = (bf16[10,256,256]{2,1,0:T(8,128)(2,1)S(1)}, bf16[10,256,256]{2,1,0:T(8,128)(2,1)S(1)}, u32[]{:S(2)}, u32[]{:S(2)}) collective-permute-start(bf16[10,256,256]{2,1,0:T(8,128)(2,1)S(1)} %get-tuple-element.19.own_ref), channel_id=1, source_target_pairs={{0,2},{2,0},{4,6},{6,4},{8,10},{10,8},{12,14},{14,12},{16,18},{18,... | collective-permute-start | bytes 3932168 | tf_op jit(solution)/shard_map/ppermute | solution.py:128
  91.7 1.3 copy-start.1
  93.1 3.0 %collective-permute-start.3 = (bf16[10,256,256]{2,1,0:T(8,128)(2,1)S(1)}, bf16[10,256,256]{2,1,0:T(8,128)(2,1)S(1)}, u32[]{:S(2)}, u32[]{:S(2)}) collective-permute-start(bf16[10,256,256]{2,1,0:T(8,128)(2,1)S(1)} %get-tuple-element.21.own_ref), channel_id=1, source_target_pairs={{0,2},{2,0},{4,6},{6,4},{8,10},{10,8},{12,14},{14,12},{16,18},{18,... | collective-permute-start | bytes 3932168 | tf_op jit(solution)/shard_map/ppermute | solution.py:128
  103.6 1.3 copy-start.3
  104.9 3.0 %collective-permute-start.4 = (bf16[10,256,256]{2,1,0:T(8,128)(2,1)S(1)}, bf16[10,256,256]{2,1,0:T(8,128)(2,1)S(1)}, u32[]{:S(2)}, u32[]{:S(2)}) collective-permute-start(bf16[10,256,256]{2,1,0:T(8,128)(2,1)S(1)} %get-tuple-element.23.own_ref), channel_id=1, source_target_pairs={{0,2},{2,0},{4,6},{6,4},{8,10},{10,8},{12,14},{14,12},{16,18},{18,... | collective-permute-start | bytes 3932168 | tf_op jit(solution)/shard_map/ppermute | solution.py:128
  115.1 5.3 %copy-start.4 = (f32[512]{0:T(512)S(1)}, f32[512]{0:T(512)}, u32[]{:S(2)}) copy-start(f32[512]{0:T(512)} %param.19) | copy-start | bytes 6148
  115.1 5.3 %copy-start.5 = (f32[512]{0:T(512)S(1)}, f32[512]{0:T(512)}, u32[]{:S(2)}) copy-start(f32[512]{0:T(512)} %param.18) | copy-start | bytes 6148
  115.1 5.3 %copy-start.6 = (f32[512]{0:T(512)S(1)}, f32[512]{0:T(512)}, u32[]{:S(2)}) copy-start(f32[512]{0:T(512)} %param.21) | copy-start | bytes 6148
  115.1 5.3 %copy-start.7 = (f32[512]{0:T(512)S(1)}, f32[512]{0:T(512)}, u32[]{:S(2)}) copy-start(f32[512]{0:T(512)} %param.20) | copy-start | bytes 6148
  115.1 53.7 %all-to-all-start.1 = ((bf16[16,128,512]{2,1,0:T(8,128)(2,1)}), bf16[16,128,512]{2,1,0:T(8,128)(2,1)S(1)}, u32[]{:S(2)}, u32[]{:S(2)}) async-start(bf16[16,128,512]{2,1,0:T(8,128)(2,1)} %shard_map.174), calls=%async_computation.1 | async-start | bytes 4194304 | tf_op jit(solution)/shard_map/all_to_all | solution.py:140

commit v2 on v1

--- a/solution.py
+++ b/solution.py
@@ -12,7 +12,8 @@
 NS_STEPS = 4
 CORES = 2
 EDGE = 256
-LIFT = 512.0
+LIFT = 2.0**25
+PACE = 2
 
 linear_coef = 3.4445
 cubic_coef = -4.775
@@ -36,6 +37,12 @@
     return (weight_new, first_new, second_new)
 
 
+def momentum_step(grads, momentum, inverse):
+    scaled = grads * inverse
+    velocity = momentum_rate * momentum.astype(jnp.float32) + scaled
+    return velocity, scaled + momentum_rate * velocity
+
+
 def span(index):
     return slice(index * EDGE, (index + 1) * EDGE)
 
@@ -77,13 +84,49 @@
                 poly[span(j), span(i)] = block.T
 
 
-def first_kernel(block_ref, turned_ref, gram_ref, *, tensor):
+def send_kernel(
+    inverse_ref, grads_ref, momentum_ref, sent_ref, sums_ref, grads, momentum, sent, sems
+):
+    matrices, rows, cols = grads.shape
+    parts = matrices // PACE
+    arrivals, departures = [], []
+    for p in range(parts):
+        part = pl.ds(p * PACE, PACE)
+        arrivals.append(
+            [
+                pltpu.make_async_copy(grads_ref.at[part], grads.at[part], sems.at[3 * p]),
+                pltpu.make_async_copy(momentum_ref.at[part], momentum.at[part], sems.at[3 * p + 1]),
+            ]
+        )
+        for copy in arrivals[-1]:
+            copy.start()
+    for p in range(parts):
+        for copy in arrivals[p]:
+            copy.wait()
+        for k in range(p * PACE, (p + 1) * PACE):
+            advance = momentum_step(grads[k], momentum[k], inverse_ref[0])[1]
+            lifted = advance * LIFT
+            sent[k] = ((lifted * lifted) * (lifted * jnp.abs(lifted))).astype(jnp.bfloat16)
+            squares = (advance * advance).reshape(rows // 8, 8, cols).sum(axis=0)
+            sums_ref[k] = sum(squares[:, c : c + 128] for c in range(0, cols, 128))
+        part = pl.ds(p * PACE, PACE)
+        departures.append(
+            pltpu.make_async_copy(sent.at[part], sent_ref.at[part], sems.at[3 * p + 2])
+        )
+        departures[-1].start()
+    for copy in departures:
+        copy.wait()
+
+
+def first_kernel(total_ref, block_ref, turned_ref, gram_ref, *, tensor):
+    scale = 1.0 / (LIFT * (jnp.sqrt(jnp.full((1, 1), total_ref[0], jnp.float32)) + norm_floor))
     blocks, rows, cols = block_ref.shape
     for s in range(blocks // tensor):
         for t in range(tensor):
-            turned_ref[t * cols : (t + 1) * cols, s * rows : (s + 1) * rows] = block_ref[
-                s * tensor + t
-            ].T
+            power = block_ref[s * tensor + t].astype(jnp.float32)
+            root = lax.rsqrt(lax.rsqrt(jnp.abs(power))) * scale
+            iterate = jnp.where(power < 0.0, -root, root).astype(jnp.bfloat16)
+            turned_ref[t * cols : (t + 1) * cols, s * rows : (s + 1) * rows] = iterate.T
     write_gram(turned_ref, gram_ref)
 
 
@@ -98,29 +141,69 @@
     write_gram(next_ref, gram_ref)
 
 
-def last_kernel(turned_ref, own_ref, other_ref, block_ref, gram, poly, *, tensor):
+def last_kernel(
+    turned_ref, own_ref, other_ref, block_ref, gram, poly, finished, sems, *, tensor, parts
+):
     write_poly(own_ref, other_ref, gram, poly)
     blocks, rows, cols = block_ref.shape
-    for s in range(blocks // tensor):
+    groups = blocks // tensor
+    copies = []
+    for s in range(groups):
         old = turned_ref[:, s * rows : (s + 1) * rows].T
         new = linear_coef * old.astype(jnp.float32) + jnp.dot(
             old, poly[...], preferred_element_type=jnp.float32
         )
         new = (math.sqrt(D) * new).astype(jnp.bfloat16)
         for t in range(tensor):
-            block_ref[s * tensor + t] = new[:, t * cols : (t + 1) * cols]
-
-
-def run_kernel(kernel, results, scratch, *operands):
+            finished[s * tensor + t] = new[:, t * cols : (t + 1) * cols]
+        if (s + 1) % (groups // parts) == 0:
+            part = pl.ds(len(copies) * (blocks // parts), blocks // parts)
+            copies.append(
+                pltpu.make_async_copy(
+                    finished.at[part], block_ref.at[part], sems.at[len(copies)]
+                )
+            )
+            copies[-1].start()
+    for copy in copies:
+        copy.wait()
+
+
+limits = pltpu.CompilerParams(vmem_limit_bytes=16 * 2**20)
+streamed = pltpu.CompilerParams(vmem_limit_bytes=60 * 2**20)
+
+
+def run_kernel(kernel, results, scratch, *operands, out=pltpu.VMEM):
     whole = pl.BlockSpec(memory_space=pltpu.VMEM)
+    scalar = pl.BlockSpec(memory_space=pltpu.SMEM)
     return pl.pallas_call(
         kernel,
         out_shape=results,
-        in_specs=[whole] * len(operands),
-        out_specs=[whole] * len(results),
+        in_specs=[scalar if value.ndim == 1 else whole for value in operands],
+        out_specs=[pl.BlockSpec(memory_space=out)] * len(results),
         scratch_shapes=scratch,
-        compiler_params=pltpu.CompilerParams(vmem_limit_bytes=48 * 2**20),
+        compiler_params=limits,
     )(*operands)
+
+
+def code(grads, momentum, inverse):
+    whole = pl.BlockSpec(memory_space=pl.ANY)
+    sent, sums = pl.pallas_call(
+        send_kernel,
+        out_shape=[
+            jax.ShapeDtypeStruct(grads.shape, jnp.bfloat16),
+            jax.ShapeDtypeStruct((grads.shape[0], 8, 128), jnp.float32),
+        ],
+        in_specs=[pl.BlockSpec(memory_space=pltpu.SMEM), whole, whole],
+        out_specs=[whole, pl.BlockSpec(memory_space=pltpu.VMEM)],
+        scratch_shapes=[
+            pltpu.VMEM(grads.shape, jnp.float32),
+            pltpu.VMEM(grads.shape, jnp.bfloat16),
+            pltpu.VMEM(grads.shape, jnp.bfloat16),
+            pltpu.SemaphoreType.DMA((3 * grads.shape[0] // PACE,)),
+        ],
+        compiler_params=streamed,
+    )(inverse.reshape(1), grads, momentum)
+    return sent, jnp.sum(sums, axis=(1, 2))
 
 
 def other_core(value):
@@ -147,7 +230,7 @@
     )
 
 
-def orthogonalize(blocks):
+def orthogonalize(blocks, total):
     tensor = lax.axis_size("tensor")
     width = tensor * blocks.shape[2]
     height = blocks.shape[0] // tensor * blocks.shape[1]
@@ -155,20 +238,32 @@
     gram_type = jax.ShapeDtypeStruct((len(upper_blocks(width)), EDGE, EDGE), jnp.bfloat16)
     squares = [pltpu.VMEM((width, width), jnp.bfloat16)] * 2
     turned, own = run_kernel(
-        functools.partial(first_kernel, tensor=tensor), [turned_type, gram_type], [], blocks
+        functools.partial(first_kernel, tensor=tensor), [turned_type, gram_type], [], total, blocks
     )
     for _ in range(NS_STEPS - 1):
         turned, own = run_kernel(
             middle_kernel, [turned_type, gram_type], squares, turned, own, other_core(own)
         )
+    parts = 4
     return run_kernel(
-        functools.partial(last_kernel, tensor=tensor),
+        functools.partial(last_kernel, tensor=tensor, parts=parts),
         [jax.ShapeDtypeStruct(blocks.shape, jnp.bfloat16)],
-        squares,
+        squares + [pltpu.VMEM(blocks.shape, jnp.bfloat16), pltpu.SemaphoreType.DMA((parts,))],
         turned,
         own,
         other_core(own),
+        out=pl.ANY,
     )[0]
+
+
+def sum_over_devices(values):
+    devices = lax.axis_size("shard") * lax.axis_size("tensor")
+    bit = 1
+    while bit < devices:
+        pairs = [(i, i ^ bit) for i in range(devices)]
+        values = values + lax.ppermute(values, ("shard", "tensor"), pairs)
+        bit *= 2
+    return values
 
 
 def body(
@@ -185,14 +280,13 @@
     gain_second,
 ):
     inverse = 1.0 / counts[0].astype(jnp.float32)
-    scaled = grads * inverse
-    velocity = momentum_rate * momentum.astype(jnp.float32) + scaled
-    advance = scaled + momentum_rate * velocity
-    owned = exchange((advance * LIFT).astype(jnp.float16)).astype(jnp.float32) / LIFT
-    total = jnp.sum(owned * owned)
-    total = jnp.sqrt(total + other_core(total))
-    iterate = (owned / (total + norm_floor)).astype(jnp.bfloat16)
-    update = exchange(orthogonalize(iterate)).astype(jnp.float32)
+    sent, sums = code(grads, momentum, inverse)
+    owned = exchange(sent)
+    grads, momentum, _ = lax.optimization_barrier((grads, momentum, sent))
+    velocity = momentum_step(grads, momentum, inverse)[0]
+    chip = lax.axis_index("shard") // CORES * lax.axis_size("tensor") + lax.axis_index("tensor")
+    total = lax.dynamic_slice_in_dim(sum_over_devices(sums), chip, 1)
+    update = exchange(orthogonalize(owned, total)).astype(jnp.float32)
     emb_new = adamw(emb_grad, emb_weight, emb_first, emb_second, inverse)
     gain_new = adamw(gain_grad, gain_weight, gain_first, gain_second, inverse)
     return (

time: 172 us -> 157 us (0.913)
  blocking collectives: 54.6 us -> 0 us
  waiting for transfers between devices: 53.1 us -> 90.2 us
  starting transfers between devices: 6.09 us -> 20.5 us
  other arithmetic: 18.2 us -> 12.5 us
  local copies, waits for them, and re-layouts: 5.27 us -> 1.59 us
    all_to_all x1 -> x0, blocking collectives: 54.6 us -> none  [exchange(): lax.all_to_all(blocks, ('shard', 'tensor'), split_axis=0, concat_axis=0,...]
    ppermute x0 -> x5, waiting for transfers between devices: none -> 39.5 us  [sum_over_devices(): values = values + lax.ppermute(values, ('shard', 'tensor'), pairs)]
    all_to_all x1 -> x2, starting transfers between devices: 5.26 us -> 13.3 us  [exchange(): lax.all_to_all(blocks, ('shard', 'tensor'), split_axis=0, concat_axis=0,...]
    ppermute x0 -> x5, starting transfers between devices: none -> 6.51 us  [sum_over_devices(): values = values + lax.ppermute(values, ('shard', 'tensor'), pairs)]
    unnamed x16 -> x18, local copies, waits for them, and re-layouts: 5.27 us -> 1.01 us
    sub x2, other arithmetic: 8.03 us -> 4.56 us  [adamw(): weight - learn_rate * (first_new / (jnp.sqrt(second_new) + adam_floor) +...]
    all_to_all x1 -> x2, waiting for transfers between devices: 40.4 us -> 39 us  [exchange(): lax.all_to_all(blocks, ('shard', 'tensor'), split_axis=0, concat_axis=0,...]
    ppermute x5 -> x4, waiting for transfers between devices: 12.7 us -> 11.7 us  [other_core(): return lax.ppermute(value, 'shard', [(i, i ^ 1) for i in range(shards)])]
  transfers between devices with their start and end apart: 6 -> 11, of which waited for: 6 -> 11; matrix products, arithmetic and copies ran while one was open for 5% -> 7% of each run, Pallas kernels for 0% -> 0%
where the time goes in v2:
time: 157 us
  waiting for transfers between devices  90.2 us (57%)
  Pallas kernels  30.8 us (20%)
  starting transfers between devices  20.5 us (13%)
  other arithmetic  12.5 us (8%)
  local copies, waits for them, and re-layouts  1.59 us (1%)
    ppermute x5, waiting for transfers between devices, sum_over_devices(): values = values + lax.ppermute(values, ('shard', 'tensor'), pairs)  39.5 us
    all_to_all x2, waiting for transfers between devices, exchange(): lax.all_to_all(blocks, ('shard', 'tensor'), split_axis=0, concat_axis=0,...  39 us
    pallas_call x5, Pallas kernels, run_kernel(): pl.pallas_call(kernel, out_shape=results, in_specs=[scalar if value.ndim...  25.9 us
    all_to_all x2, starting transfers between devices, exchange(): lax.all_to_all(blocks, ('shard', 'tensor'), split_axis=0, concat_axis=0,...  13.3 us
    ppermute x4, waiting for transfers between devices, other_core(): return lax.ppermute(value, 'shard', [(i, i ^ 1) for i in range(shards)])  11.7 us
    ppermute x5, starting transfers between devices, sum_over_devices(): values = values + lax.ppermute(values, ('shard', 'tensor'), pairs)  6.51 us
    convert_element_type x1, other arithmetic, body(): velocity.astype(jnp.bfloat16)  5.1 us
    pallas_call x1, Pallas kernels, code(): pl.pallas_call(send_kernel, out_shape=[jax.ShapeDtypeStruct(grads.shape,...  4.9 us
  transfers between devices with their start and end apart: 11, of which 11 were waited for; matrix products, arithmetic and copies ran while one was open for 7% of the time, Pallas kernels for 0%

profile of v2, /device:TPU:12, one launch (start us, length us, event | category | flops | bytes accessed | tf_op | source)
XLA Modules:
  0.0 157.0 jit_solution(16448288990685290179)
XLA Ops:
  1.3 4.9 %shard_map.170 = (bf16[16,128,512]{2,1,0:T(8,128)(2,1)}, f32[16,8,128]{2,1,0:T(8,128)}) custom-call(f32[1]{0:T(128)} %div.20.inverse_ref, f32[16,128,512]{2,1,0:T(8,128)} %grads_ref.1, bf16[16,128,512]{2,1,0:T(8,128)(2,1)} %momentum_ref.1), custom_call_target="tpu_custom_call" | custom-call | tf_op jit(solution)/shard_map/pallas_call | solution.py:190
  6.2 7.3 %all-to-all-start = ((bf16[16,128,512]{2,1,0:T(8,128)(2,1)}), bf16[16,128,512]{2,1,0:T(8,128)(2,1)S(1)}, u32[]{:S(2)}, u32[]{:S(2)}) async-start(bf16[16,128,512]{2,1,0:T(8,128)(2,1)} %get-tuple-element.20), calls=%async_computation | async-start | bytes 4194304 | tf_op jit(solution)/shard_map/all_to_all | solution.py:223
  13.8 1.5 collective-permute-start
  15.3 5.8 %collective-permute-done = f32[16]{0:T(128)S(1)} collective-permute-done((f32[16]{0:T(128)S(1)}, f32[16]{0:T(128)S(1)}, u32[]{:S(2)}, u32[]{:S(2)}) %collective-permute-start) | collective-permute-done | bytes 96 | tf_op jit(solution)/shard_map/ppermute | solution.py:264
  21.1 1.1 collective-permute-done.1
  22.2 0.6 collective-permute-start.2
  22.8 3.0 %collective-permute-done.2 = f32[16]{0:T(128)S(1)} collective-permute-done((f32[16]{0:T(128)S(1)}, f32[16]{0:T(128)S(1)}, u32[]{:S(2)}, u32[]{:S(2)}) %collective-permute-start.2) | collective-permute-done | bytes 96 | tf_op jit(solution)/shard_map/ppermute | solution.py:264
  25.7 1.5 collective-permute-start.3
  27.2 20.9 %collective-permute-done.3 = f32[16]{0:T(128)S(1)} collective-permute-done((f32[16]{0:T(128)S(1)}, f32[16]{0:T(128)S(1)}, u32[]{:S(2)}, u32[]{:S(2)}) %collective-permute-start.3) | collective-permute-done | bytes 96 | tf_op jit(solution)/shard_map/ppermute | solution.py:264
  48.2 3.0 %collective-permute-start.4 = (f32[16]{0:T(128)S(1)}, f32[16]{0:T(128)S(1)}, u32[]{:S(2)}, u32[]{:S(2)}) collective-permute-start(f32[16]{0:T(128)S(1)} %add.59), channel_id=1, source_target_pairs={{0,16},{1,17},{2,18},{3,19},{4,20},{5,21},{6,22},{7,23},{8,24},{9,... | collective-permute-start | bytes 200 | tf_op jit(solution)/shard_map/ppermute | solution.py:264
  51.1 8.6 %collective-permute-done.4 = f32[16]{0:T(128)S(1)} collective-permute-done((f32[16]{0:T(128)S(1)}, f32[16]{0:T(128)S(1)}, u32[]{:S(2)}, u32[]{:S(2)}) %collective-permute-start.4) | collective-permute-done | bytes 96 | tf_op jit(solution)/shard_map/ppermute | solution.py:264
  59.8 0.6 dynamic_slice.3.total_ref
  60.3 1.3 all-to-all-done.block_ref
  61.7 3.0 %shard_map.171 = (bf16[1024,1024]{1,0:T(8,128)(2,1)S(1)}, bf16[10,256,256]{2,1,0:T(8,128)(2,1)S(1)}) custom-call(f32[1]{0:T(128)} %dynamic_slice.3.total_ref, bf16[16,128,512]{2,1,0:T(8,128)(2,1)S(1)} %all-to-all-done.block_ref), custom_call_target="tpu_custom_call" | custom-call | tf_op jit(solution)/shard_map/pallas_call | solution.py:178
  64.7 3.0 %collective-permute-done.5.other_ref = bf16[10,256,256]{2,1,0:T(8,128)(2,1)S(1)} collective-permute-done((bf16[10,256,256]{2,1,0:T(8,128)(2,1)S(1)}, bf16[10,256,256]{2,1,0:T(8,128)(2,1)S(1)}, u32[]{:S(2)}, u32[]{:S(2)}) %collective-permute-start.5) | collective-permute-done | bytes 1310752 | tf_op jit(solution)/shard_map/ppermute | solution.py:211
  67.7 5.9 %shard_map.172 = (bf16[1024,1024]{1,0:T(8,128)(2,1)S(1)}, bf16[10,256,256]{2,1,0:T(8,128)(2,1)S(1)}) custom-call(bf16[1024,1024]{1,0:T(8,128)(2,1)S(1)} %get-tuple-element.24.turned_ref, bf16[10,256,256]{2,1,0:T(8,128)(2,1)S(1)} %get-tuple-element.25.own_ref, bf16[10,256,256]{2,1,0:T(8,128)(2,1)S(1)} %collective-permute-done.5.other_ref), custom_call_target="tpu_custom_call" | custom-call | tf_op jit(solution)/shard_map/pallas_call | solution.py:178
  73.6 0.2 collective-permute-start.6
  73.8 2.9 %collective-permute-done.6.other_ref = bf16[10,256,256]{2,1,0:T(8,128)(2,1)S(1)} collective-permute-done((bf16[10,256,256]{2,1,0:T(8,128)(2,1)S(1)}, bf16[10,256,256]{2,1,0:T(8,128)(2,1)S(1)}, u32[]{:S(2)}, u32[]{:S(2)}) %collective-permute-start.6) | collective-permute-done | bytes 1310752 | tf_op jit(solution)/shard_map/ppermute | solution.py:211
  76.7 5.9 %shard_map.173 = (bf16[1024,1024]{1,0:T(8,128)(2,1)S(1)}, bf16[10,256,256]{2,1,0:T(8,128)(2,1)S(1)}) custom-call(bf16[1024,1024]{1,0:T(8,128)(2,1)S(1)} %get-tuple-element.26.turned_ref, bf16[10,256,256]{2,1,0:T(8,128)(2,1)S(1)} %get-tuple-element.27.own_ref, bf16[10,256,256]{2,1,0:T(8,128)(2,1)S(1)} %collective-permute-done.6.other_ref), custom_call_target="tpu_custom_call" | custom-call | tf_op jit(solution)/shard_map/pallas_call | solution.py:178
  82.6 0.2 collective-permute-start.7
  82.8 2.9 %collective-permute-done.7.other_ref = bf16[10,256,256]{2,1,0:T(8,128)(2,1)S(1)} collective-permute-done((bf16[10,256,256]{2,1,0:T(8,128)(2,1)S(1)}, bf16[10,256,256]{2,1,0:T(8,128)(2,1)S(1)}, u32[]{:S(2)}, u32[]{:S(2)}) %collective-permute-start.7) | collective-permute-done | bytes 1310752 | tf_op jit(solution)/shard_map/ppermute | solution.py:211
  85.7 6.1 %shard_map.174 = (bf16[1024,1024]{1,0:T(8,128)(2,1)S(1)}, bf16[10,256,256]{2,1,0:T(8,128)(2,1)S(1)}) custom-call(bf16[1024,1024]{1,0:T(8,128)(2,1)S(1)} %get-tuple-element.28.turned_ref, bf16[10,256,256]{2,1,0:T(8,128)(2,1)S(1)} %get-tuple-element.29.own_ref, bf16[10,256,256]{2,1,0:T(8,128)(2,1)S(1)} %collective-permute-done.7.other_ref), custom_call_target="tpu_custom_call" | custom-call | tf_op jit(solution)/shard_map/pallas_call | solution.py:178
  91.9 0.2 collective-permute-start.8
  92.1 2.9 %collective-permute-done.8.other_ref = bf16[10,256,256]{2,1,0:T(8,128)(2,1)S(1)} collective-permute-done((bf16[10,256,256]{2,1,0:T(8,128)(2,1)S(1)}, bf16[10,256,256]{2,1,0:T(8,128)(2,1)S(1)}, u32[]{:S(2)}, u32[]{:S(2)}) %collective-permute-start.8) | collective-permute-done | bytes 1310752 | tf_op jit(solution)/shard_map/ppermute | solution.py:211
  95.0 5.0 %shard_map.175 = bf16[16,128,512]{2,1,0:T(8,128)(2,1)} custom-call(bf16[1024,1024]{1,0:T(8,128)(2,1)S(1)} %get-tuple-element.30.turned_ref, bf16[10,256,256]{2,1,0:T(8,128)(2,1)S(1)} %get-tuple-element.31.own_ref, bf16[10,256,256]{2,1,0:T(8,128)(2,1)S(1)} %collective-permute-done.8.other_ref), custom_call_target="tpu_custom_call" | custom-call | tf_op jit(solution)/shard_map/pallas_call | solution.py:178
  100.1 6.0 %all-to-all-start.1 = ((bf16[16,128,512]{2,1,0:T(8,128)(2,1)}), bf16[16,128,512]{2,1,0:T(8,128)(2,1)S(1)}, u32[]{:S(2)}, u32[]{:S(2)}) async-start(bf16[16,128,512]{2,1,0:T(8,128)(2,1)} %shard_map.175), calls=%async_computation.1 | async-start | bytes 4194304 | tf_op jit(solution)/shard_map/all_to_all | solution.py:223
  106.0 0.6 multiply_subtract_fusion.1
  106.7 5.1 %add_convert_fusion = bf16[16,128,512]{2,1,0:T(8,128)(2,1)} fusion(f32[16,128,512]{2,1,0:T(8,128)} %grads_ref.1, bf16[16,128,512]{2,1,0:T(8,128)(2,1)} %momentum_ref.1, f32[]{:T(128)} %bitcast), kind=kLoop, calls=%fused_computation | loop fusion | flops 5242880 | bytes 8388612 | tf_op jit(solution)/shard_map/convert_element_type | solution.py:293
  111.8 1.0 copy-done.3
  112.7 4.0 %multiply_subtract_fusion = (f32[512,1024]{1,0:T(8,128)}, f32[512,1024]{1,0:T(8,128)}, f32[512,1024]{1,0:T(8,128)}) fusion(f32[512,1024]{1,0:T(8,128)S(1)} %copy-done, f32[512,1024]{1,0:T(8,128)S(1)} %copy-done.1, f32[]{:T(128)} %bitcast, f32[512,1024]{1,0:T(8,128)S(1)} %copy-done.2, f32[512,1024]{1,0:T(8,128)S(1)} %copy-done.3), kind=kLoop, calls=%fused_computation.3 | loop fusion | flops 7340032 | bytes 14680068 | tf_op jit(solution)/shard_map/sub | solution.py:34
  116.7 37.7 %all-to-all-done.1 = bf16[16,128,512]{2,1,0:T(8,128)(2,1)S(1)} async-done(((bf16[16,128,512]{2,1,0:T(8,128)(2,1)}), bf16[16,128,512]{2,1,0:T(8,128)(2,1)S(1)}, u32[]{:S(2)}, u32[]{:S(2)}) %all-to-all-start.1) | async-done | bytes 2097184 | tf_op jit(solution)/shard_map/all_to_all | solution.py:223
  154.4 2.6 %convert_element_type.16 = f32[16,128,512]{2,1,0:T(8,128)} convert(bf16[16,128,512]{2,1,0:T(8,128)(2,1)S(1)} %all-to-all-done.1) | non-fusion elementwise | flops 1048576 | bytes 6291456 | tf_op jit(solution)/shard_map/convert_element_type | solution.py:289
  (25 shorter events, 0.3 us)
Async XLA Ops:
  6.2 7.3 %copy-start.4 = (f32[16,8,128]{2,1,0:T(8,128)S(1)}, f32[16,8,128]{2,1,0:T(8,128)}, u32[]{:S(2)}) copy-start(f32[16,8,128]{2,1,0:T(8,128)} %get-tuple-element.23) | copy-start | bytes 196612
  6.2 55.5 %all-to-all-start = ((bf16[16,128,512]{2,1,0:T(8,128)(2,1)}), bf16[16,128,512]{2,1,0:T(8,128)(2,1)S(1)}, u32[]{:S(2)}, u32[]{:S(2)}) async-start(bf16[16,128,512]{2,1,0:T(8,128)(2,1)} %get-tuple-element.20), calls=%async_computation | async-start | bytes 4194304 | tf_op jit(solution)/shard_map/all_to_all | solution.py:223
  13.8 7.3 %collective-permute-start = (f32[16]{0:T(128)S(1)}, f32[16]{0:T(128)S(1)}, u32[]{:S(2)}, u32[]{:S(2)}) collective-permute-start(f32[16]{0:T(128)S(1)} %reduce_sum.9), channel_id=1, source_target_pairs={{0,1},{1,0},{2,3},{3,2},{4,5},{5,4},{6,7},{7,6},{8,9},{9,8},{10,11... | collective-permute-start | bytes 200 | tf_op jit(solution)/shard_map/ppermute | solution.py:264
  21.1 1.1 collective-permute-start.1
  22.2 3.5 %collective-permute-start.2 = (f32[16]{0:T(128)S(1)}, f32[16]{0:T(128)S(1)}, u32[]{:S(2)}, u32[]{:S(2)}) collective-permute-start(f32[16]{0:T(128)S(1)} %add.57), channel_id=1, source_target_pairs={{0,4},{1,5},{2,6},{3,7},{4,0},{5,1},{6,2},{7,3},{8,12},{9,13},{10,... | collective-permute-start | bytes 200 | tf_op jit(solution)/shard_map/ppermute | solution.py:264
  25.7 22.4 %collective-permute-start.3 = (f32[16]{0:T(128)S(1)}, f32[16]{0:T(128)S(1)}, u32[]{:S(2)}, u32[]{:S(2)}) collective-permute-start(f32[16]{0:T(128)S(1)} %add.58), channel_id=1, source_target_pairs={{0,8},{1,9},{2,10},{3,11},{4,12},{5,13},{6,14},{7,15},{8,0},{9,1},... | collective-permute-start | bytes 200 | tf_op jit(solution)/shard_map/ppermute | solution.py:264
  48.2 11.6 %collective-permute-start.4 = (f32[16]{0:T(128)S(1)}, f32[16]{0:T(128)S(1)}, u32[]{:S(2)}, u32[]{:S(2)}) collective-permute-start(f32[16]{0:T(128)S(1)} %add.59), channel_id=1, source_target_pairs={{0,16},{1,17},{2,18},{3,19},{4,20},{5,21},{6,22},{7,23},{8,24},{9,... | collective-permute-start | bytes 200 | tf_op jit(solution)/shard_map/ppermute | solution.py:264
  64.6 3.1 %collective-permute-start.5 = (bf16[10,256,256]{2,1,0:T(8,128)(2,1)S(1)}, bf16[10,256,256]{2,1,0:T(8,128)(2,1)S(1)}, u32[]{:S(2)}, u32[]{:S(2)}) collective-permute-start(bf16[10,256,256]{2,1,0:T(8,128)(2,1)S(1)} %get-tuple-element.25.own_ref), channel_id=1, source_target_pairs={{0,2},{2,0},{4,6},{6,4},{8,10},{10,8},{12,14},{14,12},{16,18},{18,... | collective-permute-start | bytes 3932168 | tf_op jit(solution)/shard_map/ppermute | solution.py:211
  73.6 3.1 %collective-permute-start.6 = (bf16[10,256,256]{2,1,0:T(8,128)(2,1)S(1)}, bf16[10,256,256]{2,1,0:T(8,128)(2,1)S(1)}, u32[]{:S(2)}, u32[]{:S(2)}) collective-permute-start(bf16[10,256,256]{2,1,0:T(8,128)(2,1)S(1)} %get-tuple-element.27.own_ref), channel_id=1, source_target_pairs={{0,2},{2,0},{4,6},{6,4},{8,10},{10,8},{12,14},{14,12},{16,18},{18,... | collective-permute-start | bytes 3932168 | tf_op jit(solution)/shard_map/ppermute | solution.py:211
  82.6 3.1 %collective-permute-start.7 = (bf16[10,256,256]{2,1,0:T(8,128)(2,1)S(1)}, bf16[10,256,256]{2,1,0:T(8,128)(2,1)S(1)}, u32[]{:S(2)}, u32[]{:S(2)}) collective-permute-start(bf16[10,256,256]{2,1,0:T(8,128)(2,1)S(1)} %get-tuple-element.29.own_ref), channel_id=1, source_target_pairs={{0,2},{2,0},{4,6},{6,4},{8,10},{10,8},{12,14},{14,12},{16,18},{18,... | collective-permute-start | bytes 3932168 | tf_op jit(solution)/shard_map/ppermute | solution.py:211
  91.9 3.1 %collective-permute-start.8 = (bf16[10,256,256]{2,1,0:T(8,128)(2,1)S(1)}, bf16[10,256,256]{2,1,0:T(8,128)(2,1)S(1)}, u32[]{:S(2)}, u32[]{:S(2)}) collective-permute-start(bf16[10,256,256]{2,1,0:T(8,128)(2,1)S(1)} %get-tuple-element.31.own_ref), channel_id=1, source_target_pairs={{0,2},{2,0},{4,6},{6,4},{8,10},{10,8},{12,14},{14,12},{16,18},{18,... | collective-permute-start | bytes 3932168 | tf_op jit(solution)/shard_map/ppermute | solution.py:211
  100.0 6.0 %copy-start.5 = (f32[512]{0:T(512)S(1)}, f32[512]{0:T(512)}, u32[]{:S(2)}) copy-start(f32[512]{0:T(512)} %param.19) | copy-start | bytes 6148
  100.0 6.0 %copy-start.6 = (f32[512]{0:T(512)S(1)}, f32[512]{0:T(512)}, u32[]{:S(2)}) copy-start(f32[512]{0:T(512)} %param.18) | copy-start | bytes 6148
  100.0 6.0 %copy-start.7 = (f32[512]{0:T(512)S(1)}, f32[512]{0:T(512)}, u32[]{:S(2)}) copy-start(f32[512]{0:T(512)} %param.21) | copy-start | bytes 6148
  100.0 6.0 %copy-start.8 = (f32[512]{0:T(512)S(1)}, f32[512]{0:T(512)}, u32[]{:S(2)}) copy-start(f32[512]{0:T(512)} %param.20) | copy-start | bytes 6148
  100.1 54.3 %all-to-all-start.1 = ((bf16[16,128,512]{2,1,0:T(8,128)(2,1)}), bf16[16,128,512]{2,1,0:T(8,128)(2,1)S(1)}, u32[]{:S(2)}, u32[]{:S(2)}) async-start(bf16[16,128,512]{2,1,0:T(8,128)(2,1)} %shard_map.175), calls=%async_computation.1 | async-start | bytes 4194304 | tf_op jit(solution)/shard_map/all_to_all | solution.py:223
  106.7 5.1 %copy-start = (f32[512,1024]{1,0:T(8,128)S(1)}, f32[512,1024]{1,0:T(8,128)}, u32[]{:S(2)}) copy-start(f32[512,1024]{1,0:T(8,128)} %param.15) | copy-start | bytes 6291460
  106.7 5.1 %copy-start.1 = (f32[512,1024]{1,0:T(8,128)S(1)}, f32[512,1024]{1,0:T(8,128)}, u32[]{:S(2)}) copy-start(f32[512,1024]{1,0:T(8,128)} %param.14) | copy-start | bytes 6291460
  106.7 5.1 %copy-start.2 = (f32[512,1024]{1,0:T(8,128)S(1)}, f32[512,1024]{1,0:T(8,128)}, u32[]{:S(2)}) copy-start(f32[512,1024]{1,0:T(8,128)} %param.17) | copy-start | bytes 6291460
  106.7 6.1 %copy-start.3 = (f32[512,1024]{1,0:T(8,128)S(1)}, f32[512,1024]{1,0:T(8,128)}, u32[]{:S(2)}) copy-start(f32[512,1024]{1,0:T(8,128)} %param.16) | copy-start | bytes 6291460

commit v3 on v2

--- a/solution.py
+++ b/solution.py
@@ -13,6 +13,7 @@
 CORES = 2
 EDGE = 256
 LIFT = 2.0**25
+PARTS = 4
 PACE = 2
 
 linear_coef = 3.4445
@@ -37,12 +38,6 @@
     return (weight_new, first_new, second_new)
 
 
-def momentum_step(grads, momentum, inverse):
-    scaled = grads * inverse
-    velocity = momentum_rate * momentum.astype(jnp.float32) + scaled
-    return velocity, scaled + momentum_rate * velocity
-
-
 def span(index):
     return slice(index * EDGE, (index + 1) * EDGE)
 
@@ -65,28 +60,58 @@
             slot += 1
 
 
-def write_poly(own_ref, other_ref, gram, poly):
+def symmetric(left, right, finish, out):
+    for j in range(out.shape[0] // EDGE):
+        product = jnp.dot(
+            left[: (j + 1) * EDGE, :], right[:, span(j)], preferred_element_type=jnp.float32
+        )
+        for i in range(j + 1):
+            place = (span(i), span(j))
+            block = finish(place, product[span(i), :]).astype(jnp.bfloat16)
+            out[place] = block
+            if i != j:
+                out[span(j), span(i)] = block.T
+
+
+def write_factor(own_ref, other_ref, gram, poly, spare, later):
+    def read(ref, place):
+        return ref[place].astype(jnp.float32)
+
+    def polynomial(grams, out):
+        symmetric(
+            grams,
+            grams,
+            lambda place, square: cubic_coef * read(grams, place) + quintic_coef * square,
+            out,
+        )
+
     for slot, (i, j) in enumerate(upper_blocks(gram.shape[0])):
         block = own_ref[slot].astype(jnp.float32) + other_ref[slot].astype(jnp.float32)
         block = block.astype(jnp.bfloat16)
         gram[span(i), span(j)] = block
         if i != j:
             gram[span(j), span(i)] = block.T
-    for j in range(gram.shape[0] // EDGE):
-        square = jnp.dot(
-            gram[: (j + 1) * EDGE, :], gram[:, span(j)], preferred_element_type=jnp.float32
-        )
-        for i in range(j + 1):
-            block = cubic_coef * gram[span(i), span(j)].astype(jnp.float32)
-            block = (block + quintic_coef * square[span(i), :]).astype(jnp.bfloat16)
-            poly[span(i), span(j)] = block
-            if i != j:
-                poly[span(j), span(i)] = block.T
+    polynomial(gram, poly)
+    symmetric(
+        poly, poly, lambda place, square: 2.0 * linear_coef * read(poly, place) + square, spare
+    )
+    symmetric(
+        gram, spare, lambda place, change: linear_coef**2 * read(gram, place) + change, later
+    )
+    polynomial(later, gram)
+    symmetric(
+        poly,
+        gram,
+        lambda place, both: linear_coef * (read(poly, place) + read(gram, place)) + both,
+        spare,
+    )
 
 
 def send_kernel(
     inverse_ref, grads_ref, momentum_ref, sent_ref, sums_ref, grads, momentum, sent, sems
 ):
+    grad_part = LIFT * (1.0 + momentum_rate) * inverse_ref[0]
+    momentum_part = LIFT * momentum_rate**2
     matrices, rows, cols = grads.shape
     parts = matrices // PACE
     arrivals, departures = [], []
@@ -104,10 +129,10 @@
         for copy in arrivals[p]:
             copy.wait()
         for k in range(p * PACE, (p + 1) * PACE):
-            advance = momentum_step(grads[k], momentum[k], inverse_ref[0])[1]
-            lifted = advance * LIFT
-            sent[k] = ((lifted * lifted) * (lifted * jnp.abs(lifted))).astype(jnp.bfloat16)
-            squares = (advance * advance).reshape(rows // 8, 8, cols).sum(axis=0)
+            lifted = grad_part * grads[k] + momentum_part * momentum[k].astype(jnp.float32)
+            squares = lifted * lifted
+            sent[k] = (squares * (lifted * jnp.abs(lifted))).astype(jnp.bfloat16)
+            squares = squares.reshape(rows // 8, 8, cols).sum(axis=0)
             sums_ref[k] = sum(squares[:, c : c + 128] for c in range(0, cols, 128))
         part = pl.ds(p * PACE, PACE)
         departures.append(
@@ -118,8 +143,8 @@
         copy.wait()
 
 
-def first_kernel(total_ref, block_ref, turned_ref, gram_ref, *, tensor):
-    scale = 1.0 / (LIFT * (jnp.sqrt(jnp.full((1, 1), total_ref[0], jnp.float32)) + norm_floor))
+def first_kernel(totals_ref, chip_ref, block_ref, turned_ref, gram_ref, *, tensor):
+    scale = 1.0 / (jnp.sqrt(jnp.full((1, 1), totals_ref[chip_ref[0]], jnp.float32)) + LIFT * norm_floor)
     blocks, rows, cols = block_ref.shape
     for s in range(blocks // tensor):
         for t in range(tensor):
@@ -130,34 +155,34 @@
     write_gram(turned_ref, gram_ref)
 
 
-def middle_kernel(turned_ref, own_ref, other_ref, next_ref, gram_ref, gram, poly):
-    write_poly(own_ref, other_ref, gram, poly)
+def middle_kernel(turned_ref, own_ref, other_ref, next_ref, gram_ref, *squares):
+    write_factor(own_ref, other_ref, *squares)
+    factor = squares[2]
     for c in range(turned_ref.shape[1] // EDGE):
         old = turned_ref[:, span(c)]
-        new = linear_coef * old.astype(jnp.float32) + jnp.dot(
-            poly[...], old, preferred_element_type=jnp.float32
+        new = linear_coef**2 * old.astype(jnp.float32) + jnp.dot(
+            factor[...], old, preferred_element_type=jnp.float32
         )
         next_ref[:, span(c)] = new.astype(jnp.bfloat16)
     write_gram(next_ref, gram_ref)
 
 
-def last_kernel(
-    turned_ref, own_ref, other_ref, block_ref, gram, poly, finished, sems, *, tensor, parts
-):
-    write_poly(own_ref, other_ref, gram, poly)
+def last_kernel(turned_ref, own_ref, other_ref, block_ref, finished, sems, *squares, tensor):
+    write_factor(own_ref, other_ref, *squares)
+    factor = squares[2]
     blocks, rows, cols = block_ref.shape
     groups = blocks // tensor
     copies = []
     for s in range(groups):
         old = turned_ref[:, s * rows : (s + 1) * rows].T
-        new = linear_coef * old.astype(jnp.float32) + jnp.dot(
-            old, poly[...], preferred_element_type=jnp.float32
+        new = linear_coef**2 * old.astype(jnp.float32) + jnp.dot(
+            old, factor[...], preferred_element_type=jnp.float32
         )
         new = (math.sqrt(D) * new).astype(jnp.bfloat16)
         for t in range(tensor):
             finished[s * tensor + t] = new[:, t * cols : (t + 1) * cols]
-        if (s + 1) % (groups // parts) == 0:
-            part = pl.ds(len(copies) * (blocks // parts), blocks // parts)
+        if (s + 1) % (groups // PARTS) == 0:
+            part = pl.ds(len(copies) * (blocks // PARTS), blocks // PARTS)
             copies.append(
                 pltpu.make_async_copy(
                     finished.at[part], block_ref.at[part], sems.at[len(copies)]
@@ -168,7 +193,7 @@
         copy.wait()
 
 
-limits = pltpu.CompilerParams(vmem_limit_bytes=16 * 2**20)
+limits = pltpu.CompilerParams(vmem_limit_bytes=20 * 2**20)
 streamed = pltpu.CompilerParams(vmem_limit_bytes=60 * 2**20)
 
 
@@ -230,25 +255,25 @@
     )
 
 
-def orthogonalize(blocks, total):
+def orthogonalize(blocks, totals):
     tensor = lax.axis_size("tensor")
+    chip = (lax.axis_index("shard") // CORES * tensor + lax.axis_index("tensor")).reshape(1)
     width = tensor * blocks.shape[2]
     height = blocks.shape[0] // tensor * blocks.shape[1]
     turned_type = jax.ShapeDtypeStruct((width, height), jnp.bfloat16)
     gram_type = jax.ShapeDtypeStruct((len(upper_blocks(width)), EDGE, EDGE), jnp.bfloat16)
-    squares = [pltpu.VMEM((width, width), jnp.bfloat16)] * 2
+    squares = [pltpu.VMEM((width, width), jnp.bfloat16)] * 4
     turned, own = run_kernel(
-        functools.partial(first_kernel, tensor=tensor), [turned_type, gram_type], [], total, blocks
-    )
-    for _ in range(NS_STEPS - 1):
+        functools.partial(first_kernel, tensor=tensor), [turned_type, gram_type], [], totals, chip, blocks
+    )
+    for _ in range(NS_STEPS // 2 - 1):
         turned, own = run_kernel(
             middle_kernel, [turned_type, gram_type], squares, turned, own, other_core(own)
         )
-    parts = 4
     return run_kernel(
-        functools.partial(last_kernel, tensor=tensor, parts=parts),
+        functools.partial(last_kernel, tensor=tensor),
         [jax.ShapeDtypeStruct(blocks.shape, jnp.bfloat16)],
-        squares + [pltpu.VMEM(blocks.shape, jnp.bfloat16), pltpu.SemaphoreType.DMA((parts,))],
+        [pltpu.VMEM(blocks.shape, jnp.bfloat16), pltpu.SemaphoreType.DMA((PARTS,))] + squares,
         turned,
         own,
         other_core(own),
@@ -283,10 +308,8 @@
     sent, sums = code(grads, momentum, inverse)
     owned = exchange(sent)
     grads, momentum, _ = lax.optimization_barrier((grads, momentum, sent))
-    velocity = momentum_step(grads, momentum, inverse)[0]
-    chip = lax.axis_index("shard") // CORES * lax.axis_size("tensor") + lax.axis_index("tensor")
-    total = lax.dynamic_slice_in_dim(sum_over_devices(sums), chip, 1)
-    update = exchange(orthogonalize(owned, total)).astype(jnp.float32)
+    velocity = momentum_rate * momentum.astype(jnp.float32) + grads * inverse
+    update = exchange(orthogonalize(owned, sum_over_devices(sums))).astype(jnp.float32)
     emb_new = adamw(emb_grad, emb_weight, emb_first, emb_second, inverse)
     gain_new = adamw(gain_grad, gain_weight, gain_first, gain_second, inverse)
     return (

time: 157 us -> 152 us (0.968)
  waiting for transfers between devices: 90.2 us -> 85 us
    ppermute x4 -> x2, waiting for transfers between devices: 11.7 us -> 5.92 us  [other_core(): return lax.ppermute(value, 'shard', [(i, i ^ 1) for i in range(shards)])]
    pallas_call x5 -> x3, Pallas kernels: 25.9 us -> 27 us  [run_kernel(): pl.pallas_call(kernel, out_shape=results, in_specs=[scalar if value.ndim...]
  transfers between devices with their start and end apart: 11 -> 9, of which waited for: 11 -> 9; matrix products, arithmetic and copies ran while one was open for 7% -> 7% of each run, Pallas kernels for 0% -> 0%
where the time goes in v3:
time: 152 us; the launch traced here: 151 us
  waiting for transfers between devices  85 us (56%)
  Pallas kernels  31.9 us (21%)
  starting transfers between devices  19.5 us (13%)
  other arithmetic  12.5 us (8%)
    all_to_all x2, waiting for transfers between devices, exchange(): lax.all_to_all(blocks, ('shard', 'tensor'), split_axis=0, concat_axis=0,...  39.6 us
    ppermute x5, waiting for transfers between devices, sum_over_devices(): values = values + lax.ppermute(values, ('shard', 'tensor'), pairs)  39.5 us
    pallas_call x3, Pallas kernels, run_kernel(): pl.pallas_call(kernel, out_shape=results, in_specs=[scalar if value.ndim...  27 us
    all_to_all x2, starting transfers between devices, exchange(): lax.all_to_all(blocks, ('shard', 'tensor'), split_axis=0, concat_axis=0,...  12.7 us
    ppermute x5, starting transfers between devices, sum_over_devices(): values = values + lax.ppermute(values, ('shard', 'tensor'), pairs)  6.51 us
    ppermute x2, waiting for transfers between devices, other_core(): return lax.ppermute(value, 'shard', [(i, i ^ 1) for i in range(shards)])  5.92 us
    convert_element_type x1, other arithmetic, body(): velocity.astype(jnp.bfloat16)  5.1 us
    pallas_call x1, Pallas kernels, code(): pl.pallas_call(send_kernel, out_shape=[jax.ShapeDtypeStruct(grads.shape,...  4.88 us
  transfers between devices with their start and end apart: 9, of which 9 were waited for; matrix products, arithmetic and copies ran while one was open for 7% of the time, Pallas kernels for 0%

profile of v3, /device:TPU:12, one launch (start us, length us, event | category | flops | bytes accessed | tf_op | source)
XLA Modules:
  0.0 151.3 jit_solution(13567149875677203884)
XLA Ops:
  1.3 4.9 %shard_map.170 = (bf16[16,128,512]{2,1,0:T(8,128)(2,1)}, f32[16,8,128]{2,1,0:T(8,128)}) custom-call(f32[1]{0:T(128)} %div.20.inverse_ref, f32[16,128,512]{2,1,0:T(8,128)} %grads_ref.1, bf16[16,128,512]{2,1,0:T(8,128)(2,1)} %momentum_ref.1), custom_call_target="tpu_custom_call" | custom-call | tf_op jit(solution)/shard_map/pallas_call | solution.py:215
  6.2 0.0 copy-start.4
  6.2 7.3 %all-to-all-start = ((bf16[16,128,512]{2,1,0:T(8,128)(2,1)}), bf16[16,128,512]{2,1,0:T(8,128)(2,1)S(1)}, u32[]{:S(2)}, u32[]{:S(2)}) async-start(bf16[16,128,512]{2,1,0:T(8,128)(2,1)} %get-tuple-element.16), calls=%async_computation | async-start | bytes 4194304 | tf_op jit(solution)/shard_map/all_to_all | solution.py:248
  13.5 0.2 reduce_sum.9
  13.7 1.5 collective-permute-start
  15.2 5.8 %collective-permute-done = f32[16]{0:T(128)S(1)} collective-permute-done((f32[16]{0:T(128)S(1)}, f32[16]{0:T(128)S(1)}, u32[]{:S(2)}, u32[]{:S(2)}) %collective-permute-start) | collective-permute-done | bytes 96 | tf_op jit(solution)/shard_map/ppermute | solution.py:289
  21.1 1.1 collective-permute-done.1
  22.2 0.6 collective-permute-start.2
  22.8 3.0 %collective-permute-done.2 = f32[16]{0:T(128)S(1)} collective-permute-done((f32[16]{0:T(128)S(1)}, f32[16]{0:T(128)S(1)}, u32[]{:S(2)}, u32[]{:S(2)}) %collective-permute-start.2) | collective-permute-done | bytes 96 | tf_op jit(solution)/shard_map/ppermute | solution.py:289
  25.7 1.5 collective-permute-start.3
  27.2 20.9 %collective-permute-done.3 = f32[16]{0:T(128)S(1)} collective-permute-done((f32[16]{0:T(128)S(1)}, f32[16]{0:T(128)S(1)}, u32[]{:S(2)}, u32[]{:S(2)}) %collective-permute-start.3) | collective-permute-done | bytes 96 | tf_op jit(solution)/shard_map/ppermute | solution.py:289
  48.2 3.0 %collective-permute-start.4 = (f32[16]{0:T(128)S(1)}, f32[16]{0:T(128)S(1)}, u32[]{:S(2)}, u32[]{:S(2)}) collective-permute-start(f32[16]{0:T(128)S(1)} %add.56), channel_id=1, source_target_pairs={{0,16},{1,17},{2,18},{3,19},{4,20},{5,21},{6,22},{7,23},{8,24},{9,... | collective-permute-start | bytes 200 | tf_op jit(solution)/shard_map/ppermute | solution.py:289
  51.1 8.6 %collective-permute-done.4 = f32[16]{0:T(128)S(1)} collective-permute-done((f32[16]{0:T(128)S(1)}, f32[16]{0:T(128)S(1)}, u32[]{:S(2)}, u32[]{:S(2)}) %collective-permute-start.4) | collective-permute-done | bytes 96 | tf_op jit(solution)/shard_map/ppermute | solution.py:289
  59.7 1.9 %all-to-all-done.block_ref = bf16[16,128,512]{2,1,0:T(8,128)(2,1)S(1)} async-done(((bf16[16,128,512]{2,1,0:T(8,128)(2,1)}), bf16[16,128,512]{2,1,0:T(8,128)(2,1)S(1)}, u32[]{:S(2)}, u32[]{:S(2)}) %all-to-all-start) | async-done | bytes 2097184 | tf_op jit(solution)/shard_map/all_to_all | solution.py:248
  61.7 2.9 %shard_map.171 = (bf16[1024,1024]{1,0:T(8,128)(2,1)S(1)}, bf16[10,256,256]{2,1,0:T(8,128)(2,1)S(1)}) custom-call(f32[16]{0:T(128)S(1)} %add.57.totals_ref, s32[1]{0:T(128)} %bitcast.1.chip_ref, bf16[16,128,512]{2,1,0:T(8,128)(2,1)S(1)} %all-to-all-done.block_ref), custom_call_target="tpu_custom_call" | custom-call | tf_op jit(solution)/shard_map/pallas_call | solution.py:203
  64.5 0.1 collective-permute-start.5
  64.6 3.0 %collective-permute-done.5.other_ref = bf16[10,256,256]{2,1,0:T(8,128)(2,1)S(1)} collective-permute-done((bf16[10,256,256]{2,1,0:T(8,128)(2,1)S(1)}, bf16[10,256,256]{2,1,0:T(8,128)(2,1)S(1)}, u32[]{:S(2)}, u32[]{:S(2)}) %collective-permute-start.5) | collective-permute-done | bytes 1310752 | tf_op jit(solution)/shard_map/ppermute | solution.py:236
  67.6 12.3 %shard_map.172 = (bf16[1024,1024]{1,0:T(8,128)(2,1)S(1)}, bf16[10,256,256]{2,1,0:T(8,128)(2,1)S(1)}) custom-call(bf16[1024,1024]{1,0:T(8,128)(2,1)S(1)} %get-tuple-element.20.turned_ref, bf16[10,256,256]{2,1,0:T(8,128)(2,1)S(1)} %get-tuple-element.21.own_ref, bf16[10,256,256]{2,1,0:T(8,128)(2,1)S(1)} %collective-permute-done.5.other_ref), custom_call_target="tpu_custom_call" | custom-call | tf_op jit(solution)/shard_map/pallas_call | solution.py:203
  79.9 0.2 collective-permute-start.6
  80.1 2.9 %collective-permute-done.6.other_ref = bf16[10,256,256]{2,1,0:T(8,128)(2,1)S(1)} collective-permute-done((bf16[10,256,256]{2,1,0:T(8,128)(2,1)S(1)}, bf16[10,256,256]{2,1,0:T(8,128)(2,1)S(1)}, u32[]{:S(2)}, u32[]{:S(2)}) %collective-permute-start.6) | collective-permute-done | bytes 1310752 | tf_op jit(solution)/shard_map/ppermute | solution.py:236
  83.0 11.8 %shard_map.173 = bf16[16,128,512]{2,1,0:T(8,128)(2,1)} custom-call(bf16[1024,1024]{1,0:T(8,128)(2,1)S(1)} %get-tuple-element.22.turned_ref, bf16[10,256,256]{2,1,0:T(8,128)(2,1)S(1)} %get-tuple-element.23.own_ref, bf16[10,256,256]{2,1,0:T(8,128)(2,1)S(1)} %collective-permute-done.6.other_ref), custom_call_target="tpu_custom_call" | custom-call | tf_op jit(solution)/shard_map/pallas_call | solution.py:203
  94.9 0.0 copy-start.5
  94.9 0.0 copy-start.6
  94.9 0.0 copy-start.7
  94.9 0.0 copy-start.8
  94.9 5.4 %all-to-all-start.1 = ((bf16[16,128,512]{2,1,0:T(8,128)(2,1)}), bf16[16,128,512]{2,1,0:T(8,128)(2,1)S(1)}, u32[]{:S(2)}, u32[]{:S(2)}) async-start(bf16[16,128,512]{2,1,0:T(8,128)(2,1)} %shard_map.173), calls=%async_computation.1 | async-start | bytes 4194304 | tf_op jit(solution)/shard_map/all_to_all | solution.py:248
  100.3 0.6 multiply_subtract_fusion.1
  100.9 5.1 %add_convert_fusion = bf16[16,128,512]{2,1,0:T(8,128)(2,1)} fusion(f32[16,128,512]{2,1,0:T(8,128)} %grads_ref.1, bf16[16,128,512]{2,1,0:T(8,128)(2,1)} %momentum_ref.1, f32[]{:T(128)} %bitcast), kind=kLoop, calls=%fused_computation | loop fusion | flops 5242880 | bytes 8388612 | tf_op jit(solution)/shard_map/convert_element_type | solution.py:316
  106.1 1.0 copy-done.3
  107.0 4.0 %multiply_subtract_fusion = (f32[512,1024]{1,0:T(8,128)}, f32[512,1024]{1,0:T(8,128)}, f32[512,1024]{1,0:T(8,128)}) fusion(f32[512,1024]{1,0:T(8,128)S(1)} %copy-done, f32[512,1024]{1,0:T(8,128)S(1)} %copy-done.1, f32[]{:T(128)} %bitcast, f32[512,1024]{1,0:T(8,128)S(1)} %copy-done.2, f32[512,1024]{1,0:T(8,128)S(1)} %copy-done.3), kind=kLoop, calls=%fused_computation.3 | loop fusion | flops 7340032 | bytes 14680068 | tf_op jit(solution)/shard_map/sub | solution.py:35
  111.0 37.7 %all-to-all-done.1 = bf16[16,128,512]{2,1,0:T(8,128)(2,1)S(1)} async-done(((bf16[16,128,512]{2,1,0:T(8,128)(2,1)}), bf16[16,128,512]{2,1,0:T(8,128)(2,1)S(1)}, u32[]{:S(2)}, u32[]{:S(2)}) %all-to-all-start.1) | async-done | bytes 2097184 | tf_op jit(solution)/shard_map/all_to_all | solution.py:248
  148.7 2.6 %convert_element_type.16 = f32[16,128,512]{2,1,0:T(8,128)} convert(bf16[16,128,512]{2,1,0:T(8,128)(2,1)S(1)} %all-to-all-done.1) | non-fusion elementwise | flops 1048576 | bytes 6291456 | tf_op jit(solution)/shard_map/convert_element_type | solution.py:312
  (18 shorter events, 0.0 us)
Async XLA Ops:
  6.2 7.3 %copy-start.4 = (f32[16,8,128]{2,1,0:T(8,128)S(1)}, f32[16,8,128]{2,1,0:T(8,128)}, u32[]{:S(2)}) copy-start(f32[16,8,128]{2,1,0:T(8,128)} %get-tuple-element.19) | copy-start | bytes 196612
  6.2 55.5 %all-to-all-start = ((bf16[16,128,512]{2,1,0:T(8,128)(2,1)}), bf16[16,128,512]{2,1,0:T(8,128)(2,1)S(1)}, u32[]{:S(2)}, u32[]{:S(2)}) async-start(bf16[16,128,512]{2,1,0:T(8,128)(2,1)} %get-tuple-element.16), calls=%async_computation | async-start | bytes 4194304 | tf_op jit(solution)/shard_map/all_to_all | solution.py:248
  13.7 7.3 %collective-permute-start = (f32[16]{0:T(128)S(1)}, f32[16]{0:T(128)S(1)}, u32[]{:S(2)}, u32[]{:S(2)}) collective-permute-start(f32[16]{0:T(128)S(1)} %reduce_sum.9), channel_id=1, source_target_pairs={{0,1},{1,0},{2,3},{3,2},{4,5},{5,4},{6,7},{7,6},{8,9},{9,8},{10,11... | collective-permute-start | bytes 200 | tf_op jit(solution)/shard_map/ppermute | solution.py:289
  21.1 1.1 collective-permute-start.1
  22.2 3.5 %collective-permute-start.2 = (f32[16]{0:T(128)S(1)}, f32[16]{0:T(128)S(1)}, u32[]{:S(2)}, u32[]{:S(2)}) collective-permute-start(f32[16]{0:T(128)S(1)} %add.54), channel_id=1, source_target_pairs={{0,4},{1,5},{2,6},{3,7},{4,0},{5,1},{6,2},{7,3},{8,12},{9,13},{10,... | collective-permute-start | bytes 200 | tf_op jit(solution)/shard_map/ppermute | solution.py:289
  25.7 22.4 %collective-permute-start.3 = (f32[16]{0:T(128)S(1)}, f32[16]{0:T(128)S(1)}, u32[]{:S(2)}, u32[]{:S(2)}) collective-permute-start(f32[16]{0:T(128)S(1)} %add.55), channel_id=1, source_target_pairs={{0,8},{1,9},{2,10},{3,11},{4,12},{5,13},{6,14},{7,15},{8,0},{9,1},... | collective-permute-start | bytes 200 | tf_op jit(solution)/shard_map/ppermute | solution.py:289
  48.2 11.6 %collective-permute-start.4 = (f32[16]{0:T(128)S(1)}, f32[16]{0:T(128)S(1)}, u32[]{:S(2)}, u32[]{:S(2)}) collective-permute-start(f32[16]{0:T(128)S(1)} %add.56), channel_id=1, source_target_pairs={{0,16},{1,17},{2,18},{3,19},{4,20},{5,21},{6,22},{7,23},{8,24},{9,... | collective-permute-start | bytes 200 | tf_op jit(solution)/shard_map/ppermute | solution.py:289
  64.5 3.1 %collective-permute-start.5 = (bf16[10,256,256]{2,1,0:T(8,128)(2,1)S(1)}, bf16[10,256,256]{2,1,0:T(8,128)(2,1)S(1)}, u32[]{:S(2)}, u32[]{:S(2)}) collective-permute-start(bf16[10,256,256]{2,1,0:T(8,128)(2,1)S(1)} %get-tuple-element.21.own_ref), channel_id=1, source_target_pairs={{0,2},{2,0},{4,6},{6,4},{8,10},{10,8},{12,14},{14,12},{16,18},{18,... | collective-permute-start | bytes 3932168 | tf_op jit(solution)/shard_map/ppermute | solution.py:236
  79.9 3.1 %collective-permute-start.6 = (bf16[10,256,256]{2,1,0:T(8,128)(2,1)S(1)}, bf16[10,256,256]{2,1,0:T(8,128)(2,1)S(1)}, u32[]{:S(2)}, u32[]{:S(2)}) collective-permute-start(bf16[10,256,256]{2,1,0:T(8,128)(2,1)S(1)} %get-tuple-element.23.own_ref), channel_id=1, source_target_pairs={{0,2},{2,0},{4,6},{6,4},{8,10},{10,8},{12,14},{14,12},{16,18},{18,... | collective-permute-start | bytes 3932168 | tf_op jit(solution)/shard_map/ppermute | solution.py:236
  94.9 5.4 %copy-start.5 = (f32[512]{0:T(512)S(1)}, f32[512]{0:T(512)}, u32[]{:S(2)}) copy-start(f32[512]{0:T(512)} %param.19) | copy-start | bytes 6148
  94.9 5.4 %copy-start.6 = (f32[512]{0:T(512)S(1)}, f32[512]{0:T(512)}, u32[]{:S(2)}) copy-start(f32[512]{0:T(512)} %param.18) | copy-start | bytes 6148
  94.9 5.4 %copy-start.7 = (f32[512]{0:T(512)S(1)}, f32[512]{0:T(512)}, u32[]{:S(2)}) copy-start(f32[512]{0:T(512)} %param.21) | copy-start | bytes 6148
  94.9 5.4 %copy-start.8 = (f32[512]{0:T(512)S(1)}, f32[512]{0:T(512)}, u32[]{:S(2)}) copy-start(f32[512]{0:T(512)} %param.20) | copy-start | bytes 6148
  94.9 53.7 %all-to-all-start.1 = ((bf16[16,128,512]{2,1,0:T(8,128)(2,1)}), bf16[16,128,512]{2,1,0:T(8,128)(2,1)S(1)}, u32[]{:S(2)}, u32[]{:S(2)}) async-start(bf16[16,128,512]{2,1,0:T(8,128)(2,1)} %shard_map.173), calls=%async_computation.1 | async-start | bytes 4194304 | tf_op jit(solution)/shard_map/all_to_all | solution.py:248
  100.9 5.1 %copy-start = (f32[512,1024]{1,0:T(8,128)S(1)}, f32[512,1024]{1,0:T(8,128)}, u32[]{:S(2)}) copy-start(f32[512,1024]{1,0:T(8,128)} %param.15) | copy-start | bytes 6291460
  100.9 5.1 %copy-start.1 = (f32[512,1024]{1,0:T(8,128)S(1)}, f32[512,1024]{1,0:T(8,128)}, u32[]{:S(2)}) copy-start(f32[512,1024]{1,0:T(8,128)} %param.14) | copy-start | bytes 6291460
  100.9 5.1 %copy-start.2 = (f32[512,1024]{1,0:T(8,128)S(1)}, f32[512,1024]{1,0:T(8,128)}, u32[]{:S(2)}) copy-start(f32[512,1024]{1,0:T(8,128)} %param.17) | copy-start | bytes 6291460
  100.9 6.1 %copy-start.3 = (f32[512,1024]{1,0:T(8,128)S(1)}, f32[512,1024]{1,0:T(8,128)}, u32[]{:S(2)}) copy-start(f32[512,1024]{1,0:T(8,128)} %param.16) | copy-start | bytes 6291460

commit v4 on v3

--- a/solution.py
+++ b/solution.py
@@ -61,7 +61,7 @@
 
 
 def symmetric(left, right, finish, out):
-    for j in range(out.shape[0] // EDGE):
+    for j in reversed(range(out.shape[0] // EDGE)):
         product = jnp.dot(
             left[: (j + 1) * EDGE, :], right[:, span(j)], preferred_element_type=jnp.float32
         )

time: 152 us -> 149 us (0.980)
  Pallas kernels: 31.9 us -> 29.3 us
    pallas_call x3, Pallas kernels: 27 us -> 24.5 us  [run_kernel(): pl.pallas_call(kernel, out_shape=results, in_specs=[scalar if value.ndim...]
where the time goes in v4:
time: 149 us
  waiting for transfers between devices  85 us (57%)
  Pallas kernels  29.3 us (20%)
  starting transfers between devices  19.5 us (13%)
  other arithmetic  12.5 us (8%)
    all_to_all x2, waiting for transfers between devices, exchange(): lax.all_to_all(blocks, ('shard', 'tensor'), split_axis=0, concat_axis=0,...  39.6 us
    ppermute x5, waiting for transfers between devices, sum_over_devices(): values = values + lax.ppermute(values, ('shard', 'tensor'), pairs)  39.5 us
    pallas_call x3, Pallas kernels, run_kernel(): pl.pallas_call(kernel, out_shape=results, in_specs=[scalar if value.ndim...  24.5 us
    all_to_all x2, starting transfers between devices, exchange(): lax.all_to_all(blocks, ('shard', 'tensor'), split_axis=0, concat_axis=0,...  12.7 us
    ppermute x5, starting transfers between devices, sum_over_devices(): values = values + lax.ppermute(values, ('shard', 'tensor'), pairs)  6.51 us
    ppermute x2, waiting for transfers between devices, other_core(): return lax.ppermute(value, 'shard', [(i, i ^ 1) for i in range(shards)])  5.92 us
    convert_element_type x1, other arithmetic, body(): velocity.astype(jnp.bfloat16)  5.1 us
    pallas_call x1, Pallas kernels, code(): pl.pallas_call(send_kernel, out_shape=[jax.ShapeDtypeStruct(grads.shape,...  4.88 us
  transfers between devices with their start and end apart: 9, of which 9 were waited for; matrix products, arithmetic and copies ran while one was open for 7% of the time, Pallas kernels for 0%

profile of v4, /device:TPU:12, one launch (start us, length us, event | category | flops | bytes accessed | tf_op | source)
XLA Modules:
  0.0 148.7 jit_solution(4599801485645203205)
XLA Ops:
  1.3 4.9 %shard_map.170 = (bf16[16,128,512]{2,1,0:T(8,128)(2,1)}, f32[16,8,128]{2,1,0:T(8,128)}) custom-call(f32[1]{0:T(128)} %div.20.inverse_ref, f32[16,128,512]{2,1,0:T(8,128)} %grads_ref.1, bf16[16,128,512]{2,1,0:T(8,128)(2,1)} %momentum_ref.1), custom_call_target="tpu_custom_call" | custom-call | tf_op jit(solution)/shard_map/pallas_call | solution.py:215
  6.2 0.0 copy-start.4
  6.2 7.3 %all-to-all-start = ((bf16[16,128,512]{2,1,0:T(8,128)(2,1)}), bf16[16,128,512]{2,1,0:T(8,128)(2,1)S(1)}, u32[]{:S(2)}, u32[]{:S(2)}) async-start(bf16[16,128,512]{2,1,0:T(8,128)(2,1)} %get-tuple-element.16), calls=%async_computation | async-start | bytes 4194304 | tf_op jit(solution)/shard_map/all_to_all | solution.py:248
  13.5 0.2 reduce_sum.9
  13.7 1.5 %collective-permute-start = (f32[16]{0:T(128)S(1)}, f32[16]{0:T(128)S(1)}, u32[]{:S(2)}, u32[]{:S(2)}) collective-permute-start(f32[16]{0:T(128)S(1)} %reduce_sum.9), channel_id=1, source_target_pairs={{0,1},{1,0},{2,3},{3,2},{4,5},{5,4},{6,7},{7,6},{8,9},{9,8},{10,11... | collective-permute-start | bytes 200 | tf_op jit(solution)/shard_map/ppermute | solution.py:289
  15.2 5.8 %collective-permute-done = f32[16]{0:T(128)S(1)} collective-permute-done((f32[16]{0:T(128)S(1)}, f32[16]{0:T(128)S(1)}, u32[]{:S(2)}, u32[]{:S(2)}) %collective-permute-start) | collective-permute-done | bytes 96 | tf_op jit(solution)/shard_map/ppermute | solution.py:289
  21.1 1.1 collective-permute-done.1
  22.2 0.6 collective-permute-start.2
  22.8 3.0 %collective-permute-done.2 = f32[16]{0:T(128)S(1)} collective-permute-done((f32[16]{0:T(128)S(1)}, f32[16]{0:T(128)S(1)}, u32[]{:S(2)}, u32[]{:S(2)}) %collective-permute-start.2) | collective-permute-done | bytes 96 | tf_op jit(solution)/shard_map/ppermute | solution.py:289
  25.7 1.5 %collective-permute-start.3 = (f32[16]{0:T(128)S(1)}, f32[16]{0:T(128)S(1)}, u32[]{:S(2)}, u32[]{:S(2)}) collective-permute-start(f32[16]{0:T(128)S(1)} %add.55), channel_id=1, source_target_pairs={{0,8},{1,9},{2,10},{3,11},{4,12},{5,13},{6,14},{7,15},{8,0},{9,1},... | collective-permute-start | bytes 200 | tf_op jit(solution)/shard_map/ppermute | solution.py:289
  27.2 20.9 %collective-permute-done.3 = f32[16]{0:T(128)S(1)} collective-permute-done((f32[16]{0:T(128)S(1)}, f32[16]{0:T(128)S(1)}, u32[]{:S(2)}, u32[]{:S(2)}) %collective-permute-start.3) | collective-permute-done | bytes 96 | tf_op jit(solution)/shard_map/ppermute | solution.py:289
  48.2 3.0 %collective-permute-start.4 = (f32[16]{0:T(128)S(1)}, f32[16]{0:T(128)S(1)}, u32[]{:S(2)}, u32[]{:S(2)}) collective-permute-start(f32[16]{0:T(128)S(1)} %add.56), channel_id=1, source_target_pairs={{0,16},{1,17},{2,18},{3,19},{4,20},{5,21},{6,22},{7,23},{8,24},{9,... | collective-permute-start | bytes 200 | tf_op jit(solution)/shard_map/ppermute | solution.py:289
  51.1 8.6 %collective-permute-done.4 = f32[16]{0:T(128)S(1)} collective-permute-done((f32[16]{0:T(128)S(1)}, f32[16]{0:T(128)S(1)}, u32[]{:S(2)}, u32[]{:S(2)}) %collective-permute-start.4) | collective-permute-done | bytes 96 | tf_op jit(solution)/shard_map/ppermute | solution.py:289
  59.7 1.9 %all-to-all-done.block_ref = bf16[16,128,512]{2,1,0:T(8,128)(2,1)S(1)} async-done(((bf16[16,128,512]{2,1,0:T(8,128)(2,1)}), bf16[16,128,512]{2,1,0:T(8,128)(2,1)S(1)}, u32[]{:S(2)}, u32[]{:S(2)}) %all-to-all-start) | async-done | bytes 2097184 | tf_op jit(solution)/shard_map/all_to_all | solution.py:248
  61.7 2.9 %shard_map.171 = (bf16[1024,1024]{1,0:T(8,128)(2,1)S(1)}, bf16[10,256,256]{2,1,0:T(8,128)(2,1)S(1)}) custom-call(f32[16]{0:T(128)S(1)} %add.57.totals_ref, s32[1]{0:T(128)} %bitcast.1.chip_ref, bf16[16,128,512]{2,1,0:T(8,128)(2,1)S(1)} %all-to-all-done.block_ref), custom_call_target="tpu_custom_call" | custom-call | tf_op jit(solution)/shard_map/pallas_call | solution.py:203
  64.5 0.1 collective-permute-start.5
  64.6 3.0 %collective-permute-done.5.other_ref = bf16[10,256,256]{2,1,0:T(8,128)(2,1)S(1)} collective-permute-done((bf16[10,256,256]{2,1,0:T(8,128)(2,1)S(1)}, bf16[10,256,256]{2,1,0:T(8,128)(2,1)S(1)}, u32[]{:S(2)}, u32[]{:S(2)}) %collective-permute-start.5) | collective-permute-done | bytes 1310752 | tf_op jit(solution)/shard_map/ppermute | solution.py:236
  67.6 11.0 %shard_map.172 = (bf16[1024,1024]{1,0:T(8,128)(2,1)S(1)}, bf16[10,256,256]{2,1,0:T(8,128)(2,1)S(1)}) custom-call(bf16[1024,1024]{1,0:T(8,128)(2,1)S(1)} %get-tuple-element.20.turned_ref, bf16[10,256,256]{2,1,0:T(8,128)(2,1)S(1)} %get-tuple-element.21.own_ref, bf16[10,256,256]{2,1,0:T(8,128)(2,1)S(1)} %collective-permute-done.5.other_ref), custom_call_target="tpu_custom_call" | custom-call | tf_op jit(solution)/shard_map/pallas_call | solution.py:203
  78.7 0.2 collective-permute-start.6
  78.9 2.9 %collective-permute-done.6.other_ref = bf16[10,256,256]{2,1,0:T(8,128)(2,1)S(1)} collective-permute-done((bf16[10,256,256]{2,1,0:T(8,128)(2,1)S(1)}, bf16[10,256,256]{2,1,0:T(8,128)(2,1)S(1)}, u32[]{:S(2)}, u32[]{:S(2)}) %collective-permute-start.6) | collective-permute-done | bytes 1310752 | tf_op jit(solution)/shard_map/ppermute | solution.py:236
  81.8 10.6 %shard_map.173 = bf16[16,128,512]{2,1,0:T(8,128)(2,1)} custom-call(bf16[1024,1024]{1,0:T(8,128)(2,1)S(1)} %get-tuple-element.22.turned_ref, bf16[10,256,256]{2,1,0:T(8,128)(2,1)S(1)} %get-tuple-element.23.own_ref, bf16[10,256,256]{2,1,0:T(8,128)(2,1)S(1)} %collective-permute-done.6.other_ref), custom_call_target="tpu_custom_call" | custom-call | tf_op jit(solution)/shard_map/pallas_call | solution.py:203
  92.4 0.0 copy-start.5
  92.4 0.0 copy-start.6
  92.4 0.0 copy-start.7
  92.4 0.0 copy-start.8
  92.4 5.4 %all-to-all-start.1 = ((bf16[16,128,512]{2,1,0:T(8,128)(2,1)}), bf16[16,128,512]{2,1,0:T(8,128)(2,1)S(1)}, u32[]{:S(2)}, u32[]{:S(2)}) async-start(bf16[16,128,512]{2,1,0:T(8,128)(2,1)} %shard_map.173), calls=%async_computation.1 | async-start | bytes 4194304 | tf_op jit(solution)/shard_map/all_to_all | solution.py:248
  97.8 0.6 multiply_subtract_fusion.1
  98.4 5.1 %add_convert_fusion = bf16[16,128,512]{2,1,0:T(8,128)(2,1)} fusion(f32[16,128,512]{2,1,0:T(8,128)} %grads_ref.1, bf16[16,128,512]{2,1,0:T(8,128)(2,1)} %momentum_ref.1, f32[]{:T(128)} %bitcast), kind=kLoop, calls=%fused_computation | loop fusion | flops 5242880 | bytes 8388612 | tf_op jit(solution)/shard_map/convert_element_type | solution.py:316
  103.5 1.0 copy-done.3
  104.5 4.0 %multiply_subtract_fusion = (f32[512,1024]{1,0:T(8,128)}, f32[512,1024]{1,0:T(8,128)}, f32[512,1024]{1,0:T(8,128)}) fusion(f32[512,1024]{1,0:T(8,128)S(1)} %copy-done, f32[512,1024]{1,0:T(8,128)S(1)} %copy-done.1, f32[]{:T(128)} %bitcast, f32[512,1024]{1,0:T(8,128)S(1)} %copy-done.2, f32[512,1024]{1,0:T(8,128)S(1)} %copy-done.3), kind=kLoop, calls=%fused_computation.3 | loop fusion | flops 7340032 | bytes 14680068 | tf_op jit(solution)/shard_map/sub | solution.py:35
  108.5 37.7 %all-to-all-done.1 = bf16[16,128,512]{2,1,0:T(8,128)(2,1)S(1)} async-done(((bf16[16,128,512]{2,1,0:T(8,128)(2,1)}), bf16[16,128,512]{2,1,0:T(8,128)(2,1)S(1)}, u32[]{:S(2)}, u32[]{:S(2)}) %all-to-all-start.1) | async-done | bytes 2097184 | tf_op jit(solution)/shard_map/all_to_all | solution.py:248
  146.2 2.6 %convert_element_type.16 = f32[16,128,512]{2,1,0:T(8,128)} convert(bf16[16,128,512]{2,1,0:T(8,128)(2,1)S(1)} %all-to-all-done.1) | non-fusion elementwise | flops 1048576 | bytes 6291456 | tf_op jit(solution)/shard_map/convert_element_type | solution.py:312
  (18 shorter events, 0.0 us)
Async XLA Ops:
  6.2 7.3 %copy-start.4 = (f32[16,8,128]{2,1,0:T(8,128)S(1)}, f32[16,8,128]{2,1,0:T(8,128)}, u32[]{:S(2)}) copy-start(f32[16,8,128]{2,1,0:T(8,128)} %get-tuple-element.19) | copy-start | bytes 196612
  6.2 55.5 %all-to-all-start = ((bf16[16,128,512]{2,1,0:T(8,128)(2,1)}), bf16[16,128,512]{2,1,0:T(8,128)(2,1)S(1)}, u32[]{:S(2)}, u32[]{:S(2)}) async-start(bf16[16,128,512]{2,1,0:T(8,128)(2,1)} %get-tuple-element.16), calls=%async_computation | async-start | bytes 4194304 | tf_op jit(solution)/shard_map/all_to_all | solution.py:248
  13.7 7.3 %collective-permute-start = (f32[16]{0:T(128)S(1)}, f32[16]{0:T(128)S(1)}, u32[]{:S(2)}, u32[]{:S(2)}) collective-permute-start(f32[16]{0:T(128)S(1)} %reduce_sum.9), channel_id=1, source_target_pairs={{0,1},{1,0},{2,3},{3,2},{4,5},{5,4},{6,7},{7,6},{8,9},{9,8},{10,11... | collective-permute-start | bytes 200 | tf_op jit(solution)/shard_map/ppermute | solution.py:289
  21.1 1.1 collective-permute-start.1
  22.2 3.5 %collective-permute-start.2 = (f32[16]{0:T(128)S(1)}, f32[16]{0:T(128)S(1)}, u32[]{:S(2)}, u32[]{:S(2)}) collective-permute-start(f32[16]{0:T(128)S(1)} %add.54), channel_id=1, source_target_pairs={{0,4},{1,5},{2,6},{3,7},{4,0},{5,1},{6,2},{7,3},{8,12},{9,13},{10,... | collective-permute-start | bytes 200 | tf_op jit(solution)/shard_map/ppermute | solution.py:289
  25.7 22.4 %collective-permute-start.3 = (f32[16]{0:T(128)S(1)}, f32[16]{0:T(128)S(1)}, u32[]{:S(2)}, u32[]{:S(2)}) collective-permute-start(f32[16]{0:T(128)S(1)} %add.55), channel_id=1, source_target_pairs={{0,8},{1,9},{2,10},{3,11},{4,12},{5,13},{6,14},{7,15},{8,0},{9,1},... | collective-permute-start | bytes 200 | tf_op jit(solution)/shard_map/ppermute | solution.py:289
  48.2 11.6 %collective-permute-start.4 = (f32[16]{0:T(128)S(1)}, f32[16]{0:T(128)S(1)}, u32[]{:S(2)}, u32[]{:S(2)}) collective-permute-start(f32[16]{0:T(128)S(1)} %add.56), channel_id=1, source_target_pairs={{0,16},{1,17},{2,18},{3,19},{4,20},{5,21},{6,22},{7,23},{8,24},{9,... | collective-permute-start | bytes 200 | tf_op jit(solution)/shard_map/ppermute | solution.py:289
  64.5 3.1 %collective-permute-start.5 = (bf16[10,256,256]{2,1,0:T(8,128)(2,1)S(1)}, bf16[10,256,256]{2,1,0:T(8,128)(2,1)S(1)}, u32[]{:S(2)}, u32[]{:S(2)}) collective-permute-start(bf16[10,256,256]{2,1,0:T(8,128)(2,1)S(1)} %get-tuple-element.21.own_ref), channel_id=1, source_target_pairs={{0,2},{2,0},{4,6},{6,4},{8,10},{10,8},{12,14},{14,12},{16,18},{18,... | collective-permute-start | bytes 3932168 | tf_op jit(solution)/shard_map/ppermute | solution.py:236
  78.7 3.1 %collective-permute-start.6 = (bf16[10,256,256]{2,1,0:T(8,128)(2,1)S(1)}, bf16[10,256,256]{2,1,0:T(8,128)(2,1)S(1)}, u32[]{:S(2)}, u32[]{:S(2)}) collective-permute-start(bf16[10,256,256]{2,1,0:T(8,128)(2,1)S(1)} %get-tuple-element.23.own_ref), channel_id=1, source_target_pairs={{0,2},{2,0},{4,6},{6,4},{8,10},{10,8},{12,14},{14,12},{16,18},{18,... | collective-permute-start | bytes 3932168 | tf_op jit(solution)/shard_map/ppermute | solution.py:236
  92.4 5.4 %copy-start.5 = (f32[512]{0:T(512)S(1)}, f32[512]{0:T(512)}, u32[]{:S(2)}) copy-start(f32[512]{0:T(512)} %param.19) | copy-start | bytes 6148
  92.4 5.4 %copy-start.6 = (f32[512]{0:T(512)S(1)}, f32[512]{0:T(512)}, u32[]{:S(2)}) copy-start(f32[512]{0:T(512)} %param.18) | copy-start | bytes 6148
  92.4 5.4 %copy-start.7 = (f32[512]{0:T(512)S(1)}, f32[512]{0:T(512)}, u32[]{:S(2)}) copy-start(f32[512]{0:T(512)} %param.21) | copy-start | bytes 6148
  92.4 5.4 %copy-start.8 = (f32[512]{0:T(512)S(1)}, f32[512]{0:T(512)}, u32[]{:S(2)}) copy-start(f32[512]{0:T(512)} %param.20) | copy-start | bytes 6148
  92.4 53.8 %all-to-all-start.1 = ((bf16[16,128,512]{2,1,0:T(8,128)(2,1)}), bf16[16,128,512]{2,1,0:T(8,128)(2,1)S(1)}, u32[]{:S(2)}, u32[]{:S(2)}) async-start(bf16[16,128,512]{2,1,0:T(8,128)(2,1)} %shard_map.173), calls=%async_computation.1 | async-start | bytes 4194304 | tf_op jit(solution)/shard_map/all_to_all | solution.py:248
  98.4 5.1 %copy-start = (f32[512,1024]{1,0:T(8,128)S(1)}, f32[512,1024]{1,0:T(8,128)}, u32[]{:S(2)}) copy-start(f32[512,1024]{1,0:T(8,128)} %param.15) | copy-start | bytes 6291460
  98.4 5.1 %copy-start.1 = (f32[512,1024]{1,0:T(8,128)S(1)}, f32[512,1024]{1,0:T(8,128)}, u32[]{:S(2)}) copy-start(f32[512,1024]{1,0:T(8,128)} %param.14) | copy-start | bytes 6291460
  98.4 5.1 %copy-start.2 = (f32[512,1024]{1,0:T(8,128)S(1)}, f32[512,1024]{1,0:T(8,128)}, u32[]{:S(2)}) copy-start(f32[512,1024]{1,0:T(8,128)} %param.17) | copy-start | bytes 6291460
  98.4 6.1 %copy-start.3 = (f32[512,1024]{1,0:T(8,128)S(1)}, f32[512,1024]{1,0:T(8,128)}, u32[]{:S(2)}) copy-start(f32[512,1024]{1,0:T(8,128)} %param.16) | copy-start | bytes 6291460

commit v5 on v4

--- a/solution.py
+++ b/solution.py
@@ -47,8 +47,7 @@
 
 
 def write_gram(turned_ref, gram_ref):
-    slot = 0
-    for j in range(turned_ref.shape[0] // EDGE):
+    for j in reversed(range(turned_ref.shape[0] // EDGE)):
         part = lax.dot_general(
             turned_ref[: (j + 1) * EDGE, :],
             turned_ref[span(j), :],
@@ -56,8 +55,7 @@
             preferred_element_type=jnp.float32,
         )
         for i in range(j + 1):
-            gram_ref[slot] = part[span(i), :].astype(jnp.bfloat16)
-            slot += 1
+            gram_ref[j * (j + 1) // 2 + i] = part[span(i), :].astype(jnp.bfloat16)
 
 
 def symmetric(left, right, finish, out):
@@ -108,19 +106,19 @@
 
 
 def send_kernel(
-    inverse_ref, grads_ref, momentum_ref, sent_ref, sums_ref, grads, momentum, sent, sems
+    inverse_ref, grads_ref, momentum_ref, sent_ref, sums_ref, grads, momentum, sems
 ):
     grad_part = LIFT * (1.0 + momentum_rate) * inverse_ref[0]
     momentum_part = LIFT * momentum_rate**2
     matrices, rows, cols = grads.shape
     parts = matrices // PACE
-    arrivals, departures = [], []
+    arrivals = []
     for p in range(parts):
         part = pl.ds(p * PACE, PACE)
         arrivals.append(
             [
-                pltpu.make_async_copy(grads_ref.at[part], grads.at[part], sems.at[3 * p]),
-                pltpu.make_async_copy(momentum_ref.at[part], momentum.at[part], sems.at[3 * p + 1]),
+                pltpu.make_async_copy(grads_ref.at[part], grads.at[part], sems.at[2 * p]),
+                pltpu.make_async_copy(momentum_ref.at[part], momentum.at[part], sems.at[2 * p + 1]),
             ]
         )
         for copy in arrivals[-1]:
@@ -131,16 +129,9 @@
         for k in range(p * PACE, (p + 1) * PACE):
             lifted = grad_part * grads[k] + momentum_part * momentum[k].astype(jnp.float32)
             squares = lifted * lifted
-            sent[k] = (squares * (lifted * jnp.abs(lifted))).astype(jnp.bfloat16)
+            sent_ref[k] = (squares * (lifted * jnp.abs(lifted))).astype(jnp.bfloat16)
             squares = squares.reshape(rows // 8, 8, cols).sum(axis=0)
             sums_ref[k] = sum(squares[:, c : c + 128] for c in range(0, cols, 128))
-        part = pl.ds(p * PACE, PACE)
-        departures.append(
-            pltpu.make_async_copy(sent.at[part], sent_ref.at[part], sems.at[3 * p + 2])
-        )
-        departures[-1].start()
-    for copy in departures:
-        copy.wait()
 
 
 def first_kernel(totals_ref, chip_ref, block_ref, turned_ref, gram_ref, *, tensor):
@@ -148,33 +139,37 @@
     blocks, rows, cols = block_ref.shape
     for s in range(blocks // tensor):
         for t in range(tensor):
-            power = block_ref[s * tensor + t].astype(jnp.float32)
+            power = block_ref[s * tensor + t].T.astype(jnp.float32)
             root = lax.rsqrt(lax.rsqrt(jnp.abs(power))) * scale
             iterate = jnp.where(power < 0.0, -root, root).astype(jnp.bfloat16)
-            turned_ref[t * cols : (t + 1) * cols, s * rows : (s + 1) * rows] = iterate.T
+            turned_ref[t * cols : (t + 1) * cols, s * rows : (s + 1) * rows] = iterate
     write_gram(turned_ref, gram_ref)
 
 
 def middle_kernel(turned_ref, own_ref, other_ref, next_ref, gram_ref, *squares):
     write_factor(own_ref, other_ref, *squares)
     factor = squares[2]
+    for c in range(turned_ref.shape[0] // EDGE):
+        new = linear_coef**2 * turned_ref[span(c), :].astype(jnp.float32) + jnp.dot(
+            factor[span(c), :], turned_ref[...], preferred_element_type=jnp.float32
+        )
+        next_ref[span(c), :] = new.astype(jnp.bfloat16)
+    write_gram(next_ref, gram_ref)
+
+
+def flip_kernel(turned_ref, straight_ref):
     for c in range(turned_ref.shape[1] // EDGE):
-        old = turned_ref[:, span(c)]
-        new = linear_coef**2 * old.astype(jnp.float32) + jnp.dot(
-            factor[...], old, preferred_element_type=jnp.float32
-        )
-        next_ref[:, span(c)] = new.astype(jnp.bfloat16)
-    write_gram(next_ref, gram_ref)
-
-
-def last_kernel(turned_ref, own_ref, other_ref, block_ref, finished, sems, *squares, tensor):
+        straight_ref[span(c), :] = turned_ref[:, span(c)].T
+
+
+def last_kernel(straight_ref, own_ref, other_ref, block_ref, finished, sems, *squares, tensor):
     write_factor(own_ref, other_ref, *squares)
     factor = squares[2]
     blocks, rows, cols = block_ref.shape
     groups = blocks // tensor
     copies = []
     for s in range(groups):
-        old = turned_ref[:, s * rows : (s + 1) * rows].T
+        old = straight_ref[s * rows : (s + 1) * rows, :]
         new = linear_coef**2 * old.astype(jnp.float32) + jnp.dot(
             old, factor[...], preferred_element_type=jnp.float32
         )
@@ -219,12 +214,11 @@
             jax.ShapeDtypeStruct((grads.shape[0], 8, 128), jnp.float32),
         ],
         in_specs=[pl.BlockSpec(memory_space=pltpu.SMEM), whole, whole],
-        out_specs=[whole, pl.BlockSpec(memory_space=pltpu.VMEM)],
+        out_specs=[pl.BlockSpec(memory_space=pltpu.VMEM)] * 2,
         scratch_shapes=[
             pltpu.VMEM(grads.shape, jnp.float32),
             pltpu.VMEM(grads.shape, jnp.bfloat16),
-            pltpu.VMEM(grads.shape, jnp.bfloat16),
-            pltpu.SemaphoreType.DMA((3 * grads.shape[0] // PACE,)),
+            pltpu.SemaphoreType.DMA((2 * grads.shape[0] // PACE,)),
         ],
         compiler_params=streamed,
     )(inverse.reshape(1), grads, momentum)
@@ -270,11 +264,13 @@
         turned, own = run_kernel(
             middle_kernel, [turned_type, gram_type], squares, turned, own, other_core(own)
         )
+    straight_type = jax.ShapeDtypeStruct((height, width), jnp.bfloat16)
+    straight = run_kernel(flip_kernel, [straight_type], [], turned)[0]
     return run_kernel(
         functools.partial(last_kernel, tensor=tensor),
         [jax.ShapeDtypeStruct(blocks.shape, jnp.bfloat16)],
         [pltpu.VMEM(blocks.shape, jnp.bfloat16), pltpu.SemaphoreType.DMA((PARTS,))] + squares,
-        turned,
+        straight,
         own,
         other_core(own),
         out=pl.ANY,
@@ -283,11 +279,11 @@
 
 def sum_over_devices(values):
     devices = lax.axis_size("shard") * lax.axis_size("tensor")
-    bit = 1
-    while bit < devices:
+    bits = [1 << k for k in range(devices.bit_length() - 1)]
+    bits[-1] += bits[-2]
+    for bit in bits:
         pairs = [(i, i ^ bit) for i in range(devices)]
         values = values + lax.ppermute(values, ("shard", "tensor"), pairs)
-        bit *= 2
     return values
 
 

time: 149 us -> 148 us (level)
  waiting for transfers between devices: 85 us -> 83.3 us
    all_to_all x2, waiting for transfers between devices: 39.6 us -> 38 us  [exchange(): lax.all_to_all(blocks, ('shard', 'tensor'), split_axis=0, concat_axis=0,...]
    pallas_call x3 -> x4, Pallas kernels: 24.5 us -> 24.9 us  [run_kernel(): pl.pallas_call(kernel, out_shape=results, in_specs=[scalar if value.ndim...]
  transfers between devices with their start and end apart: 9 -> 9, of which waited for: 9 -> 9; matrix products, arithmetic and copies ran while one was open for 7% -> 7% of each run, Pallas kernels for 0% -> 1%
where the time goes in v5:
time: 148 us
  waiting for transfers between devices  83.3 us (56%)
  Pallas kernels  29.3 us (20%)
  starting transfers between devices  20 us (14%)
  other arithmetic  12.5 us (8%)
    ppermute x5, waiting for transfers between devices, sum_over_devices(): values = values + lax.ppermute(values, ('shard', 'tensor'), pairs)  40.2 us
    all_to_all x2, waiting for transfers between devices, exchange(): lax.all_to_all(blocks, ('shard', 'tensor'), split_axis=0, concat_axis=0,...  38 us
    pallas_call x4, Pallas kernels, run_kernel(): pl.pallas_call(kernel, out_shape=results, in_specs=[scalar if value.ndim...  24.9 us
    all_to_all x2, starting transfers between devices, exchange(): lax.all_to_all(blocks, ('shard', 'tensor'), split_axis=0, concat_axis=0,...  12.4 us
    ppermute x5, starting transfers between devices, sum_over_devices(): values = values + lax.ppermute(values, ('shard', 'tensor'), pairs)  7.4 us
    ppermute x2, waiting for transfers between devices, other_core(): return lax.ppermute(value, 'shard', [(i, i ^ 1) for i in range(shards)])  5.13 us
    convert_element_type x1, other arithmetic, body(): velocity.astype(jnp.bfloat16)  5.1 us
    sub x2, other arithmetic, adamw(): weight - learn_rate * (first_new / (jnp.sqrt(second_new) + adam_floor) +...  4.56 us
  transfers between devices with their start and end apart: 9, of which 9 were waited for; matrix products, arithmetic and copies ran while one was open for 7% of the time, Pallas kernels for 1%

profile of v5, /device:TPU:12, one launch (start us, length us, event | category | flops | bytes accessed | tf_op | source)
XLA Modules:
  0.0 147.6 jit_solution(16325245071973795331)
XLA Ops:
  1.3 4.4 %shard_map.170 = (bf16[16,128,512]{2,1,0:T(8,128)(2,1)}, f32[16,8,128]{2,1,0:T(8,128)}) custom-call(f32[1]{0:T(128)} %div.20.inverse_ref, f32[16,128,512]{2,1,0:T(8,128)} %grads_ref.1, bf16[16,128,512]{2,1,0:T(8,128)(2,1)} %momentum_ref.1), custom_call_target="tpu_custom_call" | custom-call | tf_op jit(solution)/shard_map/pallas_call | solution.py:210
  5.7 0.0 copy-start.4
  5.7 7.3 %all-to-all-start = ((bf16[16,128,512]{2,1,0:T(8,128)(2,1)}), bf16[16,128,512]{2,1,0:T(8,128)(2,1)S(1)}, u32[]{:S(2)}, u32[]{:S(2)}) async-start(bf16[16,128,512]{2,1,0:T(8,128)(2,1)} %get-tuple-element.16), calls=%async_computation | async-start | bytes 4194304 | tf_op jit(solution)/shard_map/all_to_all | solution.py:242
  13.1 0.2 reduce_sum.9
  13.3 1.5 %collective-permute-start = (f32[16]{0:T(128)S(1)}, f32[16]{0:T(128)S(1)}, u32[]{:S(2)}, u32[]{:S(2)}) collective-permute-start(f32[16]{0:T(128)S(1)} %reduce_sum.9), channel_id=1, source_target_pairs={{0,1},{1,0},{2,3},{3,2},{4,5},{5,4},{6,7},{7,6},{8,9},{9,8},{10,11... | collective-permute-start | bytes 200 | tf_op jit(solution)/shard_map/ppermute | solution.py:286
  14.8 5.8 %collective-permute-done = f32[16]{0:T(128)S(1)} collective-permute-done((f32[16]{0:T(128)S(1)}, f32[16]{0:T(128)S(1)}, u32[]{:S(2)}, u32[]{:S(2)}) %collective-permute-start) | collective-permute-done | bytes 96 | tf_op jit(solution)/shard_map/ppermute | solution.py:286
  20.6 1.1 collective-permute-done.1
  21.7 0.6 collective-permute-start.2
  22.3 3.0 %collective-permute-done.2 = f32[16]{0:T(128)S(1)} collective-permute-done((f32[16]{0:T(128)S(1)}, f32[16]{0:T(128)S(1)}, u32[]{:S(2)}, u32[]{:S(2)}) %collective-permute-start.2) | collective-permute-done | bytes 96 | tf_op jit(solution)/shard_map/ppermute | solution.py:286
  25.3 1.5 %collective-permute-start.3 = (f32[16]{0:T(128)S(1)}, f32[16]{0:T(128)S(1)}, u32[]{:S(2)}, u32[]{:S(2)}) collective-permute-start(f32[16]{0:T(128)S(1)} %add.55), channel_id=1, source_target_pairs={{0,8},{1,9},{2,10},{3,11},{4,12},{5,13},{6,14},{7,15},{8,0},{9,1},... | collective-permute-start | bytes 200 | tf_op jit(solution)/shard_map/ppermute | solution.py:286
  26.7 20.9 %collective-permute-done.3 = f32[16]{0:T(128)S(1)} collective-permute-done((f32[16]{0:T(128)S(1)}, f32[16]{0:T(128)S(1)}, u32[]{:S(2)}, u32[]{:S(2)}) %collective-permute-start.3) | collective-permute-done | bytes 96 | tf_op jit(solution)/shard_map/ppermute | solution.py:286
  47.7 3.8 %collective-permute-start.4 = (f32[16]{0:T(128)S(1)}, f32[16]{0:T(128)S(1)}, u32[]{:S(2)}, u32[]{:S(2)}) collective-permute-start(f32[16]{0:T(128)S(1)} %add.56), channel_id=1, source_target_pairs={{0,24},{1,25},{2,26},{3,27},{4,28},{5,29},{6,30},{7,31},{8,16},{9,... | collective-permute-start | bytes 200 | tf_op jit(solution)/shard_map/ppermute | solution.py:286
  51.5 9.4 %collective-permute-done.4 = f32[16]{0:T(128)S(1)} collective-permute-done((f32[16]{0:T(128)S(1)}, f32[16]{0:T(128)S(1)}, u32[]{:S(2)}, u32[]{:S(2)}) %collective-permute-start.4) | collective-permute-done | bytes 96 | tf_op jit(solution)/shard_map/ppermute | solution.py:286
  60.9 0.3 all-to-all-done.block_ref
  61.2 2.9 %shard_map.171 = (bf16[1024,1024]{1,0:T(8,128)(2,1)S(1)}, bf16[10,256,256]{2,1,0:T(8,128)(2,1)S(1)}) custom-call(f32[16]{0:T(128)S(1)} %add.57.totals_ref, s32[1]{0:T(128)} %bitcast.1.chip_ref, bf16[16,128,512]{2,1,0:T(8,128)(2,1)S(1)} %all-to-all-done.block_ref), custom_call_target="tpu_custom_call" | custom-call | tf_op jit(solution)/shard_map/pallas_call | solution.py:198
  64.1 0.1 collective-permute-start.5
  64.2 3.0 %collective-permute-done.5.other_ref = bf16[10,256,256]{2,1,0:T(8,128)(2,1)S(1)} collective-permute-done((bf16[10,256,256]{2,1,0:T(8,128)(2,1)S(1)}, bf16[10,256,256]{2,1,0:T(8,128)(2,1)S(1)}, u32[]{:S(2)}, u32[]{:S(2)}) %collective-permute-start.5) | collective-permute-done | bytes 1310752 | tf_op jit(solution)/shard_map/ppermute | solution.py:230
  67.2 10.8 %shard_map.172 = (bf16[1024,1024]{1,0:T(8,128)(2,1)S(1)}, bf16[10,256,256]{2,1,0:T(8,128)(2,1)S(1)}) custom-call(bf16[1024,1024]{1,0:T(8,128)(2,1)S(1)} %get-tuple-element.20.turned_ref, bf16[10,256,256]{2,1,0:T(8,128)(2,1)S(1)} %get-tuple-element.21.own_ref, bf16[10,256,256]{2,1,0:T(8,128)(2,1)S(1)} %collective-permute-done.5.other_ref), custom_call_target="tpu_custom_call" | custom-call | tf_op jit(solution)/shard_map/pallas_call | solution.py:198
  78.1 0.2 collective-permute-start.6
  78.3 0.8 shard_map.173.straight_ref
  79.1 2.1 %collective-permute-done.6.other_ref = bf16[10,256,256]{2,1,0:T(8,128)(2,1)S(1)} collective-permute-done((bf16[10,256,256]{2,1,0:T(8,128)(2,1)S(1)}, bf16[10,256,256]{2,1,0:T(8,128)(2,1)S(1)}, u32[]{:S(2)}, u32[]{:S(2)}) %collective-permute-start.6) | collective-permute-done | bytes 1310752 | tf_op jit(solution)/shard_map/ppermute | solution.py:230
  81.2 10.4 %shard_map.174 = bf16[16,128,512]{2,1,0:T(8,128)(2,1)} custom-call(bf16[1024,1024]{1,0:T(8,128)(2,1)S(1)} %shard_map.173.straight_ref, bf16[10,256,256]{2,1,0:T(8,128)(2,1)S(1)} %get-tuple-element.23.own_ref, bf16[10,256,256]{2,1,0:T(8,128)(2,1)S(1)} %collective-permute-done.6.other_ref), custom_call_target="tpu_custom_call" | custom-call | tf_op jit(solution)/shard_map/pallas_call | solution.py:198
  91.5 0.0 copy-start.5
  91.5 0.0 copy-start.6
  91.6 0.0 copy-start.7
  91.6 5.1 %all-to-all-start.1 = ((bf16[16,128,512]{2,1,0:T(8,128)(2,1)}), bf16[16,128,512]{2,1,0:T(8,128)(2,1)S(1)}, u32[]{:S(2)}, u32[]{:S(2)}) async-start(bf16[16,128,512]{2,1,0:T(8,128)(2,1)} %shard_map.174), calls=%async_computation.1 | async-start | bytes 4194304 | tf_op jit(solution)/shard_map/all_to_all | solution.py:242
  96.7 0.6 multiply_subtract_fusion.1
  97.3 5.1 %add_convert_fusion = bf16[16,128,512]{2,1,0:T(8,128)(2,1)} fusion(f32[16,128,512]{2,1,0:T(8,128)} %grads_ref.1, bf16[16,128,512]{2,1,0:T(8,128)(2,1)} %momentum_ref.1, f32[]{:T(128)} %bitcast), kind=kLoop, calls=%fused_computation | loop fusion | flops 5242880 | bytes 8388612 | tf_op jit(solution)/shard_map/convert_element_type | solution.py:312
  102.4 1.0 copy-done.3
  103.4 4.0 %multiply_subtract_fusion = (f32[512,1024]{1,0:T(8,128)}, f32[512,1024]{1,0:T(8,128)}, f32[512,1024]{1,0:T(8,128)}) fusion(f32[512,1024]{1,0:T(8,128)S(1)} %copy-done, f32[512,1024]{1,0:T(8,128)S(1)} %copy-done.1, f32[]{:T(128)} %bitcast, f32[512,1024]{1,0:T(8,128)S(1)} %copy-done.2, f32[512,1024]{1,0:T(8,128)S(1)} %copy-done.3), kind=kLoop, calls=%fused_computation.3 | loop fusion | flops 7340032 | bytes 14680068 | tf_op jit(solution)/shard_map/sub | solution.py:35
  107.3 37.7 %all-to-all-done.1 = bf16[16,128,512]{2,1,0:T(8,128)(2,1)S(1)} async-done(((bf16[16,128,512]{2,1,0:T(8,128)(2,1)}), bf16[16,128,512]{2,1,0:T(8,128)(2,1)S(1)}, u32[]{:S(2)}, u32[]{:S(2)}) %all-to-all-start.1) | async-done | bytes 2097184 | tf_op jit(solution)/shard_map/all_to_all | solution.py:242
  145.0 2.6 %convert_element_type.16 = f32[16,128,512]{2,1,0:T(8,128)} convert(bf16[16,128,512]{2,1,0:T(8,128)(2,1)S(1)} %all-to-all-done.1) | non-fusion elementwise | flops 1048576 | bytes 6291456 | tf_op jit(solution)/shard_map/convert_element_type | solution.py:308
  (19 shorter events, 0.0 us)
Async XLA Ops:
  5.7 7.3 %copy-start.4 = (f32[16,8,128]{2,1,0:T(8,128)S(1)}, f32[16,8,128]{2,1,0:T(8,128)}, u32[]{:S(2)}) copy-start(f32[16,8,128]{2,1,0:T(8,128)} %get-tuple-element.19) | copy-start | bytes 196612
  5.7 55.5 %all-to-all-start = ((bf16[16,128,512]{2,1,0:T(8,128)(2,1)}), bf16[16,128,512]{2,1,0:T(8,128)(2,1)S(1)}, u32[]{:S(2)}, u32[]{:S(2)}) async-start(bf16[16,128,512]{2,1,0:T(8,128)(2,1)} %get-tuple-element.16), calls=%async_computation | async-start | bytes 4194304 | tf_op jit(solution)/shard_map/all_to_all | solution.py:242
  13.3 7.3 %collective-permute-start = (f32[16]{0:T(128)S(1)}, f32[16]{0:T(128)S(1)}, u32[]{:S(2)}, u32[]{:S(2)}) collective-permute-start(f32[16]{0:T(128)S(1)} %reduce_sum.9), channel_id=1, source_target_pairs={{0,1},{1,0},{2,3},{3,2},{4,5},{5,4},{6,7},{7,6},{8,9},{9,8},{10,11... | collective-permute-start | bytes 200 | tf_op jit(solution)/shard_map/ppermute | solution.py:286
  20.6 1.1 collective-permute-start.1
  21.7 3.5 %collective-permute-start.2 = (f32[16]{0:T(128)S(1)}, f32[16]{0:T(128)S(1)}, u32[]{:S(2)}, u32[]{:S(2)}) collective-permute-start(f32[16]{0:T(128)S(1)} %add.54), channel_id=1, source_target_pairs={{0,4},{1,5},{2,6},{3,7},{4,0},{5,1},{6,2},{7,3},{8,12},{9,13},{10,... | collective-permute-start | bytes 200 | tf_op jit(solution)/shard_map/ppermute | solution.py:286
  25.3 22.4 %collective-permute-start.3 = (f32[16]{0:T(128)S(1)}, f32[16]{0:T(128)S(1)}, u32[]{:S(2)}, u32[]{:S(2)}) collective-permute-start(f32[16]{0:T(128)S(1)} %add.55), channel_id=1, source_target_pairs={{0,8},{1,9},{2,10},{3,11},{4,12},{5,13},{6,14},{7,15},{8,0},{9,1},... | collective-permute-start | bytes 200 | tf_op jit(solution)/shard_map/ppermute | solution.py:286
  47.7 13.2 %collective-permute-start.4 = (f32[16]{0:T(128)S(1)}, f32[16]{0:T(128)S(1)}, u32[]{:S(2)}, u32[]{:S(2)}) collective-permute-start(f32[16]{0:T(128)S(1)} %add.56), channel_id=1, source_target_pairs={{0,24},{1,25},{2,26},{3,27},{4,28},{5,29},{6,30},{7,31},{8,16},{9,... | collective-permute-start | bytes 200 | tf_op jit(solution)/shard_map/ppermute | solution.py:286
  64.1 3.1 %collective-permute-start.5 = (bf16[10,256,256]{2,1,0:T(8,128)(2,1)S(1)}, bf16[10,256,256]{2,1,0:T(8,128)(2,1)S(1)}, u32[]{:S(2)}, u32[]{:S(2)}) collective-permute-start(bf16[10,256,256]{2,1,0:T(8,128)(2,1)S(1)} %get-tuple-element.21.own_ref), channel_id=1, source_target_pairs={{0,2},{2,0},{4,6},{6,4},{8,10},{10,8},{12,14},{14,12},{16,18},{18,... | collective-permute-start | bytes 3932168 | tf_op jit(solution)/shard_map/ppermute | solution.py:230
  78.1 3.1 %collective-permute-start.6 = (bf16[10,256,256]{2,1,0:T(8,128)(2,1)S(1)}, bf16[10,256,256]{2,1,0:T(8,128)(2,1)S(1)}, u32[]{:S(2)}, u32[]{:S(2)}) collective-permute-start(bf16[10,256,256]{2,1,0:T(8,128)(2,1)S(1)} %get-tuple-element.23.own_ref), channel_id=1, source_target_pairs={{0,2},{2,0},{4,6},{6,4},{8,10},{10,8},{12,14},{14,12},{16,18},{18,... | collective-permute-start | bytes 3932168 | tf_op jit(solution)/shard_map/ppermute | solution.py:230
  91.5 5.1 %copy-start.5 = (f32[512]{0:T(512)S(1)}, f32[512]{0:T(512)}, u32[]{:S(2)}) copy-start(f32[512]{0:T(512)} %param.19) | copy-start | bytes 6148
  91.5 5.1 %copy-start.6 = (f32[512]{0:T(512)S(1)}, f32[512]{0:T(512)}, u32[]{:S(2)}) copy-start(f32[512]{0:T(512)} %param.18) | copy-start | bytes 6148
  91.6 5.1 %copy-start.7 = (f32[512]{0:T(512)S(1)}, f32[512]{0:T(512)}, u32[]{:S(2)}) copy-start(f32[512]{0:T(512)} %param.21) | copy-start | bytes 6148
  91.6 5.1 %copy-start.8 = (f32[512]{0:T(512)S(1)}, f32[512]{0:T(512)}, u32[]{:S(2)}) copy-start(f32[512]{0:T(512)} %param.20) | copy-start | bytes 6148
  91.6 53.4 %all-to-all-start.1 = ((bf16[16,128,512]{2,1,0:T(8,128)(2,1)}), bf16[16,128,512]{2,1,0:T(8,128)(2,1)S(1)}, u32[]{:S(2)}, u32[]{:S(2)}) async-start(bf16[16,128,512]{2,1,0:T(8,128)(2,1)} %shard_map.174), calls=%async_computation.1 | async-start | bytes 4194304 | tf_op jit(solution)/shard_map/all_to_all | solution.py:242
  97.3 5.1 %copy-start = (f32[512,1024]{1,0:T(8,128)S(1)}, f32[512,1024]{1,0:T(8,128)}, u32[]{:S(2)}) copy-start(f32[512,1024]{1,0:T(8,128)} %param.15) | copy-start | bytes 6291460
  97.3 5.1 %copy-start.1 = (f32[512,1024]{1,0:T(8,128)S(1)}, f32[512,1024]{1,0:T(8,128)}, u32[]{:S(2)}) copy-start(f32[512,1024]{1,0:T(8,128)} %param.14) | copy-start | bytes 6291460
  97.3 5.1 %copy-start.2 = (f32[512,1024]{1,0:T(8,128)S(1)}, f32[512,1024]{1,0:T(8,128)}, u32[]{:S(2)}) copy-start(f32[512,1024]{1,0:T(8,128)} %param.17) | copy-start | bytes 6291460
  97.3 6.1 %copy-start.3 = (f32[512,1024]{1,0:T(8,128)S(1)}, f32[512,1024]{1,0:T(8,128)}, u32[]{:S(2)}) copy-start(f32[512,1024]{1,0:T(8,128)} %param.16) | copy-start | bytes 6291460

commit v6 on v5

--- a/solution.py
+++ b/solution.py
@@ -166,24 +166,25 @@
     write_factor(own_ref, other_ref, *squares)
     factor = squares[2]
     blocks, rows, cols = block_ref.shape
-    groups = blocks // tensor
+    height = straight_ref.shape[0]
     copies = []
-    for s in range(groups):
-        old = straight_ref[s * rows : (s + 1) * rows, :]
+    for p in range(PARTS):
+        top, bottom = p * height // PARTS, (p + 1) * height // PARTS
+        old = straight_ref[top:bottom, :]
         new = linear_coef**2 * old.astype(jnp.float32) + jnp.dot(
             old, factor[...], preferred_element_type=jnp.float32
         )
         new = (math.sqrt(D) * new).astype(jnp.bfloat16)
-        for t in range(tensor):
-            finished[s * tensor + t] = new[:, t * cols : (t + 1) * cols]
-        if (s + 1) % (groups // PARTS) == 0:
-            part = pl.ds(len(copies) * (blocks // PARTS), blocks // PARTS)
-            copies.append(
-                pltpu.make_async_copy(
-                    finished.at[part], block_ref.at[part], sems.at[len(copies)]
-                )
-            )
-            copies[-1].start()
+        for s in range(top // rows, bottom // rows):
+            for t in range(tensor):
+                finished[s * tensor + t] = new[
+                    s * rows - top : (s + 1) * rows - top, t * cols : (t + 1) * cols
+                ]
+        part = pl.ds(p * (blocks // PARTS), blocks // PARTS)
+        copies.append(
+            pltpu.make_async_copy(finished.at[part], block_ref.at[part], sems.at[p])
+        )
+        copies[-1].start()
     for copy in copies:
         copy.wait()
 

time: 148 us -> 148 us (level)
  no operation moved by 1% of the time
where the time goes in v6:
time: 148 us
  waiting for transfers between devices  83.3 us (56%)
  Pallas kernels  29.3 us (20%)
  starting transfers between devices  20 us (14%)
  other arithmetic  12.5 us (8%)
    ppermute x5, waiting for transfers between devices, sum_over_devices(): values = values + lax.ppermute(values, ('shard', 'tensor'), pairs)  40.2 us
    all_to_all x2, waiting for transfers between devices, exchange(): lax.all_to_all(blocks, ('shard', 'tensor'), split_axis=0, concat_axis=0,...  38 us
    pallas_call x4, Pallas kernels, run_kernel(): pl.pallas_call(kernel, out_shape=results, in_specs=[scalar if value.ndim...  24.9 us
    all_to_all x2, starting transfers between devices, exchange(): lax.all_to_all(blocks, ('shard', 'tensor'), split_axis=0, concat_axis=0,...  12.4 us
    ppermute x5, starting transfers between devices, sum_over_devices(): values = values + lax.ppermute(values, ('shard', 'tensor'), pairs)  7.4 us
    ppermute x2, waiting for transfers between devices, other_core(): return lax.ppermute(value, 'shard', [(i, i ^ 1) for i in range(shards)])  5.13 us
    convert_element_type x1, other arithmetic, body(): velocity.astype(jnp.bfloat16)  5.1 us
    sub x2, other arithmetic, adamw(): weight - learn_rate * (first_new / (jnp.sqrt(second_new) + adam_floor) +...  4.56 us
  transfers between devices with their start and end apart: 9, of which 9 were waited for; matrix products, arithmetic and copies ran while one was open for 7% of the time, Pallas kernels for 1%

profile of v6, /device:TPU:12, one launch (start us, length us, event | category | flops | bytes accessed | tf_op | source)
XLA Modules:
  0.0 147.6 jit_solution(12657533854061002165)
XLA Ops:
  1.3 4.4 %shard_map.170 = (bf16[16,128,512]{2,1,0:T(8,128)(2,1)}, f32[16,8,128]{2,1,0:T(8,128)}) custom-call(f32[1]{0:T(128)} %div.20.inverse_ref, f32[16,128,512]{2,1,0:T(8,128)} %grads_ref.1, bf16[16,128,512]{2,1,0:T(8,128)(2,1)} %momentum_ref.1), custom_call_target="tpu_custom_call" | custom-call | tf_op jit(solution)/shard_map/pallas_call | solution.py:211
  5.7 0.0 copy-start.4
  5.7 7.3 %all-to-all-start = ((bf16[16,128,512]{2,1,0:T(8,128)(2,1)}), bf16[16,128,512]{2,1,0:T(8,128)(2,1)S(1)}, u32[]{:S(2)}, u32[]{:S(2)}) async-start(bf16[16,128,512]{2,1,0:T(8,128)(2,1)} %get-tuple-element.16), calls=%async_computation | async-start | bytes 4194304 | tf_op jit(solution)/shard_map/all_to_all | solution.py:243
  13.1 0.2 reduce_sum.9
  13.3 1.5 %collective-permute-start = (f32[16]{0:T(128)S(1)}, f32[16]{0:T(128)S(1)}, u32[]{:S(2)}, u32[]{:S(2)}) collective-permute-start(f32[16]{0:T(128)S(1)} %reduce_sum.9), channel_id=1, source_target_pairs={{0,1},{1,0},{2,3},{3,2},{4,5},{5,4},{6,7},{7,6},{8,9},{9,8},{10,11... | collective-permute-start | bytes 200 | tf_op jit(solution)/shard_map/ppermute | solution.py:287
  14.8 5.8 %collective-permute-done = f32[16]{0:T(128)S(1)} collective-permute-done((f32[16]{0:T(128)S(1)}, f32[16]{0:T(128)S(1)}, u32[]{:S(2)}, u32[]{:S(2)}) %collective-permute-start) | collective-permute-done | bytes 96 | tf_op jit(solution)/shard_map/ppermute | solution.py:287
  20.6 1.1 collective-permute-done.1
  21.7 0.6 collective-permute-start.2
  22.3 3.0 %collective-permute-done.2 = f32[16]{0:T(128)S(1)} collective-permute-done((f32[16]{0:T(128)S(1)}, f32[16]{0:T(128)S(1)}, u32[]{:S(2)}, u32[]{:S(2)}) %collective-permute-start.2) | collective-permute-done | bytes 96 | tf_op jit(solution)/shard_map/ppermute | solution.py:287
  25.3 1.5 %collective-permute-start.3 = (f32[16]{0:T(128)S(1)}, f32[16]{0:T(128)S(1)}, u32[]{:S(2)}, u32[]{:S(2)}) collective-permute-start(f32[16]{0:T(128)S(1)} %add.55), channel_id=1, source_target_pairs={{0,8},{1,9},{2,10},{3,11},{4,12},{5,13},{6,14},{7,15},{8,0},{9,1},... | collective-permute-start | bytes 200 | tf_op jit(solution)/shard_map/ppermute | solution.py:287
  26.7 20.9 %collective-permute-done.3 = f32[16]{0:T(128)S(1)} collective-permute-done((f32[16]{0:T(128)S(1)}, f32[16]{0:T(128)S(1)}, u32[]{:S(2)}, u32[]{:S(2)}) %collective-permute-start.3) | collective-permute-done | bytes 96 | tf_op jit(solution)/shard_map/ppermute | solution.py:287
  47.7 3.8 %collective-permute-start.4 = (f32[16]{0:T(128)S(1)}, f32[16]{0:T(128)S(1)}, u32[]{:S(2)}, u32[]{:S(2)}) collective-permute-start(f32[16]{0:T(128)S(1)} %add.56), channel_id=1, source_target_pairs={{0,24},{1,25},{2,26},{3,27},{4,28},{5,29},{6,30},{7,31},{8,16},{9,... | collective-permute-start | bytes 200 | tf_op jit(solution)/shard_map/ppermute | solution.py:287
  51.5 9.4 %collective-permute-done.4 = f32[16]{0:T(128)S(1)} collective-permute-done((f32[16]{0:T(128)S(1)}, f32[16]{0:T(128)S(1)}, u32[]{:S(2)}, u32[]{:S(2)}) %collective-permute-start.4) | collective-permute-done | bytes 96 | tf_op jit(solution)/shard_map/ppermute | solution.py:287
  60.9 0.3 all-to-all-done.block_ref
  61.2 2.9 %shard_map.171 = (bf16[1024,1024]{1,0:T(8,128)(2,1)S(1)}, bf16[10,256,256]{2,1,0:T(8,128)(2,1)S(1)}) custom-call(f32[16]{0:T(128)S(1)} %add.57.totals_ref, s32[1]{0:T(128)} %bitcast.1.chip_ref, bf16[16,128,512]{2,1,0:T(8,128)(2,1)S(1)} %all-to-all-done.block_ref), custom_call_target="tpu_custom_call" | custom-call | tf_op jit(solution)/shard_map/pallas_call | solution.py:199
  64.1 0.1 collective-permute-start.5
  64.2 3.0 %collective-permute-done.5.other_ref = bf16[10,256,256]{2,1,0:T(8,128)(2,1)S(1)} collective-permute-done((bf16[10,256,256]{2,1,0:T(8,128)(2,1)S(1)}, bf16[10,256,256]{2,1,0:T(8,128)(2,1)S(1)}, u32[]{:S(2)}, u32[]{:S(2)}) %collective-permute-start.5) | collective-permute-done | bytes 1310752 | tf_op jit(solution)/shard_map/ppermute | solution.py:231
  67.2 10.8 %shard_map.172 = (bf16[1024,1024]{1,0:T(8,128)(2,1)S(1)}, bf16[10,256,256]{2,1,0:T(8,128)(2,1)S(1)}) custom-call(bf16[1024,1024]{1,0:T(8,128)(2,1)S(1)} %get-tuple-element.20.turned_ref, bf16[10,256,256]{2,1,0:T(8,128)(2,1)S(1)} %get-tuple-element.21.own_ref, bf16[10,256,256]{2,1,0:T(8,128)(2,1)S(1)} %collective-permute-done.5.other_ref), custom_call_target="tpu_custom_call" | custom-call | tf_op jit(solution)/shard_map/pallas_call | solution.py:199
  78.1 0.2 collective-permute-start.6
  78.3 0.8 shard_map.173.straight_ref
  79.1 2.1 %collective-permute-done.6.other_ref = bf16[10,256,256]{2,1,0:T(8,128)(2,1)S(1)} collective-permute-done((bf16[10,256,256]{2,1,0:T(8,128)(2,1)S(1)}, bf16[10,256,256]{2,1,0:T(8,128)(2,1)S(1)}, u32[]{:S(2)}, u32[]{:S(2)}) %collective-permute-start.6) | collective-permute-done | bytes 1310752 | tf_op jit(solution)/shard_map/ppermute | solution.py:231
  81.2 10.4 %shard_map.174 = bf16[16,128,512]{2,1,0:T(8,128)(2,1)} custom-call(bf16[1024,1024]{1,0:T(8,128)(2,1)S(1)} %shard_map.173.straight_ref, bf16[10,256,256]{2,1,0:T(8,128)(2,1)S(1)} %get-tuple-element.23.own_ref, bf16[10,256,256]{2,1,0:T(8,128)(2,1)S(1)} %collective-permute-done.6.other_ref), custom_call_target="tpu_custom_call" | custom-call | tf_op jit(solution)/shard_map/pallas_call | solution.py:199
  91.5 0.0 copy-start.5
  91.5 0.0 copy-start.6
  91.5 0.0 copy-start.7
  91.6 5.1 %all-to-all-start.1 = ((bf16[16,128,512]{2,1,0:T(8,128)(2,1)}), bf16[16,128,512]{2,1,0:T(8,128)(2,1)S(1)}, u32[]{:S(2)}, u32[]{:S(2)}) async-start(bf16[16,128,512]{2,1,0:T(8,128)(2,1)} %shard_map.174), calls=%async_computation.1 | async-start | bytes 4194304 | tf_op jit(solution)/shard_map/all_to_all | solution.py:243
  96.7 0.6 multiply_subtract_fusion.1
  97.3 5.1 %add_convert_fusion = bf16[16,128,512]{2,1,0:T(8,128)(2,1)} fusion(f32[16,128,512]{2,1,0:T(8,128)} %grads_ref.1, bf16[16,128,512]{2,1,0:T(8,128)(2,1)} %momentum_ref.1, f32[]{:T(128)} %bitcast), kind=kLoop, calls=%fused_computation | loop fusion | flops 5242880 | bytes 8388612 | tf_op jit(solution)/shard_map/convert_element_type | solution.py:313
  102.4 1.0 copy-done.3
  103.4 4.0 %multiply_subtract_fusion = (f32[512,1024]{1,0:T(8,128)}, f32[512,1024]{1,0:T(8,128)}, f32[512,1024]{1,0:T(8,128)}) fusion(f32[512,1024]{1,0:T(8,128)S(1)} %copy-done, f32[512,1024]{1,0:T(8,128)S(1)} %copy-done.1, f32[]{:T(128)} %bitcast, f32[512,1024]{1,0:T(8,128)S(1)} %copy-done.2, f32[512,1024]{1,0:T(8,128)S(1)} %copy-done.3), kind=kLoop, calls=%fused_computation.3 | loop fusion | flops 7340032 | bytes 14680068 | tf_op jit(solution)/shard_map/sub | solution.py:35
  107.3 37.7 %all-to-all-done.1 = bf16[16,128,512]{2,1,0:T(8,128)(2,1)S(1)} async-done(((bf16[16,128,512]{2,1,0:T(8,128)(2,1)}), bf16[16,128,512]{2,1,0:T(8,128)(2,1)S(1)}, u32[]{:S(2)}, u32[]{:S(2)}) %all-to-all-start.1) | async-done | bytes 2097184 | tf_op jit(solution)/shard_map/all_to_all | solution.py:243
  145.0 2.6 %convert_element_type.16 = f32[16,128,512]{2,1,0:T(8,128)} convert(bf16[16,128,512]{2,1,0:T(8,128)(2,1)S(1)} %all-to-all-done.1) | non-fusion elementwise | flops 1048576 | bytes 6291456 | tf_op jit(solution)/shard_map/convert_element_type | solution.py:309
  (19 shorter events, 0.0 us)
Async XLA Ops:
  5.7 7.3 %copy-start.4 = (f32[16,8,128]{2,1,0:T(8,128)S(1)}, f32[16,8,128]{2,1,0:T(8,128)}, u32[]{:S(2)}) copy-start(f32[16,8,128]{2,1,0:T(8,128)} %get-tuple-element.19) | copy-start | bytes 196612
  5.7 55.5 %all-to-all-start = ((bf16[16,128,512]{2,1,0:T(8,128)(2,1)}), bf16[16,128,512]{2,1,0:T(8,128)(2,1)S(1)}, u32[]{:S(2)}, u32[]{:S(2)}) async-start(bf16[16,128,512]{2,1,0:T(8,128)(2,1)} %get-tuple-element.16), calls=%async_computation | async-start | bytes 4194304 | tf_op jit(solution)/shard_map/all_to_all | solution.py:243
  13.3 7.3 %collective-permute-start = (f32[16]{0:T(128)S(1)}, f32[16]{0:T(128)S(1)}, u32[]{:S(2)}, u32[]{:S(2)}) collective-permute-start(f32[16]{0:T(128)S(1)} %reduce_sum.9), channel_id=1, source_target_pairs={{0,1},{1,0},{2,3},{3,2},{4,5},{5,4},{6,7},{7,6},{8,9},{9,8},{10,11... | collective-permute-start | bytes 200 | tf_op jit(solution)/shard_map/ppermute | solution.py:287
  20.6 1.1 collective-permute-start.1
  21.7 3.5 %collective-permute-start.2 = (f32[16]{0:T(128)S(1)}, f32[16]{0:T(128)S(1)}, u32[]{:S(2)}, u32[]{:S(2)}) collective-permute-start(f32[16]{0:T(128)S(1)} %add.54), channel_id=1, source_target_pairs={{0,4},{1,5},{2,6},{3,7},{4,0},{5,1},{6,2},{7,3},{8,12},{9,13},{10,... | collective-permute-start | bytes 200 | tf_op jit(solution)/shard_map/ppermute | solution.py:287
  25.3 22.4 %collective-permute-start.3 = (f32[16]{0:T(128)S(1)}, f32[16]{0:T(128)S(1)}, u32[]{:S(2)}, u32[]{:S(2)}) collective-permute-start(f32[16]{0:T(128)S(1)} %add.55), channel_id=1, source_target_pairs={{0,8},{1,9},{2,10},{3,11},{4,12},{5,13},{6,14},{7,15},{8,0},{9,1},... | collective-permute-start | bytes 200 | tf_op jit(solution)/shard_map/ppermute | solution.py:287
  47.7 13.2 %collective-permute-start.4 = (f32[16]{0:T(128)S(1)}, f32[16]{0:T(128)S(1)}, u32[]{:S(2)}, u32[]{:S(2)}) collective-permute-start(f32[16]{0:T(128)S(1)} %add.56), channel_id=1, source_target_pairs={{0,24},{1,25},{2,26},{3,27},{4,28},{5,29},{6,30},{7,31},{8,16},{9,... | collective-permute-start | bytes 200 | tf_op jit(solution)/shard_map/ppermute | solution.py:287
  64.1 3.1 %collective-permute-start.5 = (bf16[10,256,256]{2,1,0:T(8,128)(2,1)S(1)}, bf16[10,256,256]{2,1,0:T(8,128)(2,1)S(1)}, u32[]{:S(2)}, u32[]{:S(2)}) collective-permute-start(bf16[10,256,256]{2,1,0:T(8,128)(2,1)S(1)} %get-tuple-element.21.own_ref), channel_id=1, source_target_pairs={{0,2},{2,0},{4,6},{6,4},{8,10},{10,8},{12,14},{14,12},{16,18},{18,... | collective-permute-start | bytes 3932168 | tf_op jit(solution)/shard_map/ppermute | solution.py:231
  78.1 3.1 %collective-permute-start.6 = (bf16[10,256,256]{2,1,0:T(8,128)(2,1)S(1)}, bf16[10,256,256]{2,1,0:T(8,128)(2,1)S(1)}, u32[]{:S(2)}, u32[]{:S(2)}) collective-permute-start(bf16[10,256,256]{2,1,0:T(8,128)(2,1)S(1)} %get-tuple-element.23.own_ref), channel_id=1, source_target_pairs={{0,2},{2,0},{4,6},{6,4},{8,10},{10,8},{12,14},{14,12},{16,18},{18,... | collective-permute-start | bytes 3932168 | tf_op jit(solution)/shard_map/ppermute | solution.py:231
  91.5 5.1 %copy-start.5 = (f32[512]{0:T(512)S(1)}, f32[512]{0:T(512)}, u32[]{:S(2)}) copy-start(f32[512]{0:T(512)} %param.19) | copy-start | bytes 6148
  91.5 5.1 %copy-start.6 = (f32[512]{0:T(512)S(1)}, f32[512]{0:T(512)}, u32[]{:S(2)}) copy-start(f32[512]{0:T(512)} %param.18) | copy-start | bytes 6148
  91.5 5.1 %copy-start.7 = (f32[512]{0:T(512)S(1)}, f32[512]{0:T(512)}, u32[]{:S(2)}) copy-start(f32[512]{0:T(512)} %param.21) | copy-start | bytes 6148
  91.6 5.1 %copy-start.8 = (f32[512]{0:T(512)S(1)}, f32[512]{0:T(512)}, u32[]{:S(2)}) copy-start(f32[512]{0:T(512)} %param.20) | copy-start | bytes 6148
  91.6 53.4 %all-to-all-start.1 = ((bf16[16,128,512]{2,1,0:T(8,128)(2,1)}), bf16[16,128,512]{2,1,0:T(8,128)(2,1)S(1)}, u32[]{:S(2)}, u32[]{:S(2)}) async-start(bf16[16,128,512]{2,1,0:T(8,128)(2,1)} %shard_map.174), calls=%async_computation.1 | async-start | bytes 4194304 | tf_op jit(solution)/shard_map/all_to_all | solution.py:243
  97.3 5.1 %copy-start = (f32[512,1024]{1,0:T(8,128)S(1)}, f32[512,1024]{1,0:T(8,128)}, u32[]{:S(2)}) copy-start(f32[512,1024]{1,0:T(8,128)} %param.15) | copy-start | bytes 6291460
  97.3 5.1 %copy-start.1 = (f32[512,1024]{1,0:T(8,128)S(1)}, f32[512,1024]{1,0:T(8,128)}, u32[]{:S(2)}) copy-start(f32[512,1024]{1,0:T(8,128)} %param.14) | copy-start | bytes 6291460
  97.3 5.1 %copy-start.2 = (f32[512,1024]{1,0:T(8,128)S(1)}, f32[512,1024]{1,0:T(8,128)}, u32[]{:S(2)}) copy-start(f32[512,1024]{1,0:T(8,128)} %param.17) | copy-start | bytes 6291460
  97.3 6.1 %copy-start.3 = (f32[512,1024]{1,0:T(8,128)S(1)}, f32[512,1024]{1,0:T(8,128)}, u32[]{:S(2)}) copy-start(f32[512,1024]{1,0:T(8,128)} %param.16) | copy-start | bytes 6291460

commit v7 on v5

--- a/solution.py
+++ b/solution.py
@@ -305,11 +305,13 @@
     owned = exchange(sent)
     grads, momentum, _ = lax.optimization_barrier((grads, momentum, sent))
     velocity = momentum_rate * momentum.astype(jnp.float32) + grads * inverse
+    emb_new = adamw(emb_grad, emb_weight, emb_first, emb_second, inverse)
+    momentum_new = velocity.astype(jnp.bfloat16)
+    owned, momentum_new, emb_new = lax.optimization_barrier((owned, momentum_new, emb_new))
     update = exchange(orthogonalize(owned, sum_over_devices(sums))).astype(jnp.float32)
-    emb_new = adamw(emb_grad, emb_weight, emb_first, emb_second, inverse)
     gain_new = adamw(gain_grad, gain_weight, gain_first, gain_second, inverse)
     return (
-        velocity.astype(jnp.bfloat16),
+        momentum_new,
         update,
         emb_new[0],
         emb_new[1],

time: 148 us -> 148 us (level)
    all_to_all x2, waiting for transfers between devices: 38 us -> 48 us  [exchange(): lax.all_to_all(blocks, ('shard', 'tensor'), split_axis=0, concat_axis=0,...]
    ppermute x5, waiting for transfers between devices: 40.2 us -> 31.1 us  [sum_over_devices(): values = values + lax.ppermute(values, ('shard', 'tensor'), pairs)]
  transfers between devices with their start and end apart: 9 -> 9, of which waited for: 9 -> 8; matrix products, arithmetic and copies ran while one was open for 7% -> 7% of each run, Pallas kernels for 1% -> 0%
where the time goes in v7:
time: 148 us
  waiting for transfers between devices  84.4 us (57%)
  Pallas kernels  29.3 us (20%)
  starting transfers between devices  19.1 us (13%)
  other arithmetic  12.5 us (8%)
    all_to_all x2, waiting for transfers between devices, exchange(): lax.all_to_all(blocks, ('shard', 'tensor'), split_axis=0, concat_axis=0,...  48 us
    ppermute x5, waiting for transfers between devices, sum_over_devices(): values = values + lax.ppermute(values, ('shard', 'tensor'), pairs)  31.1 us
    pallas_call x4, Pallas kernels, run_kernel(): pl.pallas_call(kernel, out_shape=results, in_specs=[scalar if value.ndim...  24.9 us
    all_to_all x2, starting transfers between devices, exchange(): lax.all_to_all(blocks, ('shard', 'tensor'), split_axis=0, concat_axis=0,...  12.4 us
    ppermute x5, starting transfers between devices, sum_over_devices(): values = values + lax.ppermute(values, ('shard', 'tensor'), pairs)  6.48 us
    ppermute x2, waiting for transfers between devices, other_core(): return lax.ppermute(value, 'shard', [(i, i ^ 1) for i in range(shards)])  5.3 us
    convert_element_type x1, other arithmetic, body(): momentum_new = velocity.astype(jnp.bfloat16)  5.1 us
    sub x2, other arithmetic, adamw(): weight - learn_rate * (first_new / (jnp.sqrt(second_new) + adam_floor) +...  4.56 us
  transfers between devices with their start and end apart: 9, of which 8 were waited for; matrix products, arithmetic and copies ran while one was open for 7% of the time, Pallas kernels for 0%

profile of v7, /device:TPU:12, one launch (start us, length us, event | category | flops | bytes accessed | tf_op | source)
XLA Modules:
  0.0 147.8 jit_solution(7453339638345468226)
XLA Ops:
  1.3 4.4 %shard_map.170 = (bf16[16,128,512]{2,1,0:T(8,128)(2,1)}, f32[16,8,128]{2,1,0:T(8,128)}) custom-call(f32[1]{0:T(128)} %div.20.inverse_ref, f32[16,128,512]{2,1,0:T(8,128)} %grads_ref.1, bf16[16,128,512]{2,1,0:T(8,128)(2,1)} %momentum_ref.1), custom_call_target="tpu_custom_call" | custom-call | tf_op jit(solution)/shard_map/pallas_call | solution.py:210
  5.7 0.0 copy-start.4
  5.7 7.3 %all-to-all-start = ((bf16[16,128,512]{2,1,0:T(8,128)(2,1)}), bf16[16,128,512]{2,1,0:T(8,128)(2,1)S(1)}, u32[]{:S(2)}, u32[]{:S(2)}) async-start(bf16[16,128,512]{2,1,0:T(8,128)(2,1)} %get-tuple-element.21), calls=%async_computation | async-start | bytes 4194304 | tf_op jit(solution)/shard_map/all_to_all | solution.py:242
  13.1 0.2 reduce_sum.9
  13.3 1.5 %collective-permute-start = (f32[16]{0:T(128)S(1)}, f32[16]{0:T(128)S(1)}, u32[]{:S(2)}, u32[]{:S(2)}) collective-permute-start(f32[16]{0:T(128)S(1)} %reduce_sum.9), channel_id=1, source_target_pairs={{0,1},{1,0},{2,3},{3,2},{4,5},{5,4},{6,7},{7,6},{8,9},{9,8},{10,11... | collective-permute-start | bytes 200 | tf_op jit(solution)/shard_map/ppermute | solution.py:286
  14.8 5.1 %add_convert_fusion = bf16[16,128,512]{2,1,0:T(8,128)(2,1)} fusion(f32[16,128,512]{2,1,0:T(8,128)} %grads_ref.1, bf16[16,128,512]{2,1,0:T(8,128)(2,1)} %momentum_ref.1, f32[]{:T(128)} %bitcast), kind=kLoop, calls=%fused_computation | loop fusion | flops 5242880 | bytes 8388612 | tf_op jit(solution)/shard_map/convert_element_type | solution.py:309
  19.9 1.0 copy-done.3
  20.9 4.0 %multiply_subtract_fusion = (f32[512,1024]{1,0:T(8,128)}, f32[512,1024]{1,0:T(8,128)}, f32[512,1024]{1,0:T(8,128)}) fusion(f32[512,1024]{1,0:T(8,128)S(1)} %copy-done, f32[512,1024]{1,0:T(8,128)S(1)} %copy-done.1, f32[]{:T(128)} %bitcast, f32[512,1024]{1,0:T(8,128)S(1)} %copy-done.2, f32[512,1024]{1,0:T(8,128)S(1)} %copy-done.3), kind=kLoop, calls=%fused_computation.3 | loop fusion | flops 7340032 | bytes 14680068 | tf_op jit(solution)/shard_map/sub | solution.py:35
  24.8 1.1 collective-permute-done.1
  25.9 0.6 collective-permute-start.2
  26.5 3.0 %collective-permute-done.2 = f32[16]{0:T(128)S(1)} collective-permute-done((f32[16]{0:T(128)S(1)}, f32[16]{0:T(128)S(1)}, u32[]{:S(2)}, u32[]{:S(2)}) %collective-permute-start.2) | collective-permute-done | bytes 96 | tf_op jit(solution)/shard_map/ppermute | solution.py:286
  29.5 0.6 collective-permute-start.3
  30.0 17.6 %collective-permute-done.3 = f32[16]{0:T(128)S(1)} collective-permute-done((f32[16]{0:T(128)S(1)}, f32[16]{0:T(128)S(1)}, u32[]{:S(2)}, u32[]{:S(2)}) %collective-permute-start.3) | collective-permute-done | bytes 96 | tf_op jit(solution)/shard_map/ppermute | solution.py:286
  47.7 3.8 %collective-permute-start.4 = (f32[16]{0:T(128)S(1)}, f32[16]{0:T(128)S(1)}, u32[]{:S(2)}, u32[]{:S(2)}) collective-permute-start(f32[16]{0:T(128)S(1)} %add.61), channel_id=1, source_target_pairs={{0,24},{1,25},{2,26},{3,27},{4,28},{5,29},{6,30},{7,31},{8,16},{9,... | collective-permute-start | bytes 200 | tf_op jit(solution)/shard_map/ppermute | solution.py:286
  51.5 9.4 %collective-permute-done.4 = f32[16]{0:T(128)S(1)} collective-permute-done((f32[16]{0:T(128)S(1)}, f32[16]{0:T(128)S(1)}, u32[]{:S(2)}, u32[]{:S(2)}) %collective-permute-start.4) | collective-permute-done | bytes 96 | tf_op jit(solution)/shard_map/ppermute | solution.py:286
  60.9 0.3 all-to-all-done.block_ref
  61.2 2.9 %shard_map.171 = (bf16[1024,1024]{1,0:T(8,128)(2,1)S(1)}, bf16[10,256,256]{2,1,0:T(8,128)(2,1)S(1)}) custom-call(f32[16]{0:T(128)S(1)} %add.62.totals_ref, s32[1]{0:T(128)} %bitcast.1.chip_ref, bf16[16,128,512]{2,1,0:T(8,128)(2,1)S(1)} %all-to-all-done.block_ref), custom_call_target="tpu_custom_call" | custom-call | tf_op jit(solution)/shard_map/pallas_call | solution.py:198
  64.1 0.1 collective-permute-start.5
  64.2 3.0 %collective-permute-done.5.other_ref = bf16[10,256,256]{2,1,0:T(8,128)(2,1)S(1)} collective-permute-done((bf16[10,256,256]{2,1,0:T(8,128)(2,1)S(1)}, bf16[10,256,256]{2,1,0:T(8,128)(2,1)S(1)}, u32[]{:S(2)}, u32[]{:S(2)}) %collective-permute-start.5) | collective-permute-done | bytes 1310752 | tf_op jit(solution)/shard_map/ppermute | solution.py:230
  67.2 11.0 %shard_map.172 = (bf16[1024,1024]{1,0:T(8,128)(2,1)S(1)}, bf16[10,256,256]{2,1,0:T(8,128)(2,1)S(1)}) custom-call(bf16[1024,1024]{1,0:T(8,128)(2,1)S(1)} %get-tuple-element.27.turned_ref, bf16[10,256,256]{2,1,0:T(8,128)(2,1)S(1)} %get-tuple-element.28.own_ref, bf16[10,256,256]{2,1,0:T(8,128)(2,1)S(1)} %collective-permute-done.5.other_ref), custom_call_target="tpu_custom_call" | custom-call | tf_op jit(solution)/shard_map/pallas_call | solution.py:198
  78.2 0.2 collective-permute-start.6
  78.4 0.6 shard_map.173.straight_ref
  79.1 2.3 %collective-permute-done.6.other_ref = bf16[10,256,256]{2,1,0:T(8,128)(2,1)S(1)} collective-permute-done((bf16[10,256,256]{2,1,0:T(8,128)(2,1)S(1)}, bf16[10,256,256]{2,1,0:T(8,128)(2,1)S(1)}, u32[]{:S(2)}, u32[]{:S(2)}) %collective-permute-start.6) | collective-permute-done | bytes 1310752 | tf_op jit(solution)/shard_map/ppermute | solution.py:230
  81.3 10.4 %shard_map.174 = bf16[16,128,512]{2,1,0:T(8,128)(2,1)} custom-call(bf16[1024,1024]{1,0:T(8,128)(2,1)S(1)} %shard_map.173.straight_ref, bf16[10,256,256]{2,1,0:T(8,128)(2,1)S(1)} %get-tuple-element.30.own_ref, bf16[10,256,256]{2,1,0:T(8,128)(2,1)S(1)} %collective-permute-done.6.other_ref), custom_call_target="tpu_custom_call" | custom-call | tf_op jit(solution)/shard_map/pallas_call | solution.py:198
  91.7 0.0 copy-start.5
  91.7 0.0 copy-start.6
  91.7 0.0 copy-start.7
  91.8 0.0 copy-start.8
  91.8 5.1 %all-to-all-start.1 = ((bf16[16,128,512]{2,1,0:T(8,128)(2,1)}), bf16[16,128,512]{2,1,0:T(8,128)(2,1)S(1)}, u32[]{:S(2)}, u32[]{:S(2)}) async-start(bf16[16,128,512]{2,1,0:T(8,128)(2,1)} %shard_map.174), calls=%async_computation.1 | async-start | bytes 4194304 | tf_op jit(solution)/shard_map/all_to_all | solution.py:242
  96.9 0.6 multiply_subtract_fusion.1
  97.5 47.7 %all-to-all-done.1 = bf16[16,128,512]{2,1,0:T(8,128)(2,1)S(1)} async-done(((bf16[16,128,512]{2,1,0:T(8,128)(2,1)}), bf16[16,128,512]{2,1,0:T(8,128)(2,1)S(1)}, u32[]{:S(2)}, u32[]{:S(2)}) %all-to-all-start.1) | async-done | bytes 2097184 | tf_op jit(solution)/shard_map/all_to_all | solution.py:242
  145.2 2.6 %convert_element_type.16 = f32[16,128,512]{2,1,0:T(8,128)} convert(bf16[16,128,512]{2,1,0:T(8,128)(2,1)S(1)} %all-to-all-done.1) | non-fusion elementwise | flops 1048576 | bytes 6291456 | tf_op jit(solution)/shard_map/convert_element_type | solution.py:311
  (19 shorter events, 0.0 us)
Async XLA Ops:
  5.7 7.3 %copy-start.4 = (f32[16,8,128]{2,1,0:T(8,128)S(1)}, f32[16,8,128]{2,1,0:T(8,128)}, u32[]{:S(2)}) copy-start(f32[16,8,128]{2,1,0:T(8,128)} %get-tuple-element.25) | copy-start | bytes 196612
  5.7 55.5 %all-to-all-start = ((bf16[16,128,512]{2,1,0:T(8,128)(2,1)}), bf16[16,128,512]{2,1,0:T(8,128)(2,1)S(1)}, u32[]{:S(2)}, u32[]{:S(2)}) async-start(bf16[16,128,512]{2,1,0:T(8,128)(2,1)} %get-tuple-element.21), calls=%async_computation | async-start | bytes 4194304 | tf_op jit(solution)/shard_map/all_to_all | solution.py:242
  13.3 11.6 %collective-permute-start = (f32[16]{0:T(128)S(1)}, f32[16]{0:T(128)S(1)}, u32[]{:S(2)}, u32[]{:S(2)}) collective-permute-start(f32[16]{0:T(128)S(1)} %reduce_sum.9), channel_id=1, source_target_pairs={{0,1},{1,0},{2,3},{3,2},{4,5},{5,4},{6,7},{7,6},{8,9},{9,8},{10,11... | collective-permute-start | bytes 200 | tf_op jit(solution)/shard_map/ppermute | solution.py:286
  14.8 5.1 %copy-start = (f32[512,1024]{1,0:T(8,128)S(1)}, f32[512,1024]{1,0:T(8,128)}, u32[]{:S(2)}) copy-start(f32[512,1024]{1,0:T(8,128)} %param.15) | copy-start | bytes 6291460
  14.8 5.1 %copy-start.1 = (f32[512,1024]{1,0:T(8,128)S(1)}, f32[512,1024]{1,0:T(8,128)}, u32[]{:S(2)}) copy-start(f32[512,1024]{1,0:T(8,128)} %param.14) | copy-start | bytes 6291460
  14.8 5.1 %copy-start.2 = (f32[512,1024]{1,0:T(8,128)S(1)}, f32[512,1024]{1,0:T(8,128)}, u32[]{:S(2)}) copy-start(f32[512,1024]{1,0:T(8,128)} %param.17) | copy-start | bytes 6291460
  14.8 6.1 %copy-start.3 = (f32[512,1024]{1,0:T(8,128)S(1)}, f32[512,1024]{1,0:T(8,128)}, u32[]{:S(2)}) copy-start(f32[512,1024]{1,0:T(8,128)} %param.16) | copy-start | bytes 6291460
  24.8 1.1 collective-permute-start.1
  25.9 3.5 %collective-permute-start.2 = (f32[16]{0:T(128)S(1)}, f32[16]{0:T(128)S(1)}, u32[]{:S(2)}, u32[]{:S(2)}) collective-permute-start(f32[16]{0:T(128)S(1)} %add.59), channel_id=1, source_target_pairs={{0,4},{1,5},{2,6},{3,7},{4,0},{5,1},{6,2},{7,3},{8,12},{9,13},{10,... | collective-permute-start | bytes 200 | tf_op jit(solution)/shard_map/ppermute | solution.py:286
  29.5 18.2 %collective-permute-start.3 = (f32[16]{0:T(128)S(1)}, f32[16]{0:T(128)S(1)}, u32[]{:S(2)}, u32[]{:S(2)}) collective-permute-start(f32[16]{0:T(128)S(1)} %add.60), channel_id=1, source_target_pairs={{0,8},{1,9},{2,10},{3,11},{4,12},{5,13},{6,14},{7,15},{8,0},{9,1},... | collective-permute-start | bytes 200 | tf_op jit(solution)/shard_map/ppermute | solution.py:286
  47.7 13.2 %collective-permute-start.4 = (f32[16]{0:T(128)S(1)}, f32[16]{0:T(128)S(1)}, u32[]{:S(2)}, u32[]{:S(2)}) collective-permute-start(f32[16]{0:T(128)S(1)} %add.61), channel_id=1, source_target_pairs={{0,24},{1,25},{2,26},{3,27},{4,28},{5,29},{6,30},{7,31},{8,16},{9,... | collective-permute-start | bytes 200 | tf_op jit(solution)/shard_map/ppermute | solution.py:286
  64.1 3.1 %collective-permute-start.5 = (bf16[10,256,256]{2,1,0:T(8,128)(2,1)S(1)}, bf16[10,256,256]{2,1,0:T(8,128)(2,1)S(1)}, u32[]{:S(2)}, u32[]{:S(2)}) collective-permute-start(bf16[10,256,256]{2,1,0:T(8,128)(2,1)S(1)} %get-tuple-element.28.own_ref), channel_id=1, source_target_pairs={{0,2},{2,0},{4,6},{6,4},{8,10},{10,8},{12,14},{14,12},{16,18},{18,... | collective-permute-start | bytes 3932168 | tf_op jit(solution)/shard_map/ppermute | solution.py:230
  78.2 3.1 %collective-permute-start.6 = (bf16[10,256,256]{2,1,0:T(8,128)(2,1)S(1)}, bf16[10,256,256]{2,1,0:T(8,128)(2,1)S(1)}, u32[]{:S(2)}, u32[]{:S(2)}) collective-permute-start(bf16[10,256,256]{2,1,0:T(8,128)(2,1)S(1)} %get-tuple-element.30.own_ref), channel_id=1, source_target_pairs={{0,2},{2,0},{4,6},{6,4},{8,10},{10,8},{12,14},{14,12},{16,18},{18,... | collective-permute-start | bytes 3932168 | tf_op jit(solution)/shard_map/ppermute | solution.py:230
  91.7 5.1 %copy-start.5 = (f32[512]{0:T(512)S(1)}, f32[512]{0:T(512)}, u32[]{:S(2)}) copy-start(f32[512]{0:T(512)} %param.19) | copy-start | bytes 6148
  91.7 5.1 %copy-start.6 = (f32[512]{0:T(512)S(1)}, f32[512]{0:T(512)}, u32[]{:S(2)}) copy-start(f32[512]{0:T(512)} %param.18) | copy-start | bytes 6148
  91.7 5.1 %copy-start.7 = (f32[512]{0:T(512)S(1)}, f32[512]{0:T(512)}, u32[]{:S(2)}) copy-start(f32[512]{0:T(512)} %param.21) | copy-start | bytes 6148
  91.8 5.1 %copy-start.8 = (f32[512]{0:T(512)S(1)}, f32[512]{0:T(512)}, u32[]{:S(2)}) copy-start(f32[512]{0:T(512)} %param.20) | copy-start | bytes 6148
  91.8 53.4 %all-to-all-start.1 = ((bf16[16,128,512]{2,1,0:T(8,128)(2,1)}), bf16[16,128,512]{2,1,0:T(8,128)(2,1)S(1)}, u32[]{:S(2)}, u32[]{:S(2)}) async-start(bf16[16,128,512]{2,1,0:T(8,128)(2,1)} %shard_map.174), calls=%async_computation.1 | async-start | bytes 4194304 | tf_op jit(solution)/shard_map/all_to_all | solution.py:242
